TPU v7x, 128 devices: a whole 4x4x4 slice. The times are simulated.
128 devices in a mesh: band: 4 (over z_hi, core), dom: 32 (over z_lo, y, x).
Axes of the slice: x: 4, y: 4, z: 4 (z_hi: 2, z_lo: 2; z = z_hi * 2 + z_lo), core: 2. Of those that a mesh axis runs over, the one named last changes fastest.
Arguments:
- orbitals: float32 [8, 256, 512, 512], P('band', 'dom'), may hold values from -6 to 6
- occupation: int32 [8], P('band'), may hold values from 500 to 2000
- core_density: float32 [256, 512, 512], P('dom', 'band'), may hold values from 0.05 to 0.5
- proj_values: float32 [2048, 8, 128], P('dom'), may hold values from -1.5 to 1.5
- block_index: int32 [2048, 128], P('dom'), may hold values from 0 to 2097151, as said below
- live_points: int32 [2048], P('dom'), may hold values from 32 to 128
Outputs:
- potential: float32 [256, 512, 512], P('dom', 'band')
Inputs may be any that keep to these rules, and one draw needn't show every extreme that they name: `block_index`: a flat index into any of the 2097152 cells of the block's own domain.
All inputs are finite; a program needn't handle non-finite values.
Results may differ from a plain program's by a relative error of at most 0.0003.
Values sent between devices are 32-bit elements; how exact they have to be, the bound alone decides.
A program may use at most 128 MiB of HBM per device.

v0:
```python
import math

import jax
import jax.numpy as jnp
from jax import lax
from jax.sharding import PartitionSpec as P

coef_a = 0.75 * (3.0 / math.pi) ** (1.0 / 3.0)
kappa_val = 0.804
mu_val = 0.2195149727645171
s_scale = 4.0 * (3.0 * math.pi**2) ** (2.0 / 3.0)


def padded(cells, sides, width):
    for axis, dim in sides:
        count = lax.axis_size(axis)
        head = lax.slice_in_dim(cells, 0, width, axis=dim)
        tail = lax.slice_in_dim(cells, cells.shape[dim] - width, cells.shape[dim], axis=dim)
        cells = jnp.concatenate(
            [
                lax.ppermute(tail, axis, [(i, (i + 1) % count) for i in range(count)]),
                cells,
                lax.ppermute(head, axis, [((i + 1) % count, i) for i in range(count)]),
            ],
            axis=dim,
        )
    return cells


def energy_density(density, sigma):
    n_four = density * jnp.cbrt(density)
    reduced = sigma / (s_scale * n_four * n_four)
    factor = 1.0 + kappa_val - kappa_val / (1.0 + mu_val * reduced / kappa_val)
    return -coef_a * n_four * factor


def xc_parts(density, sigma):
    _, pull = jax.vjp(energy_density, density, sigma)
    return pull(jnp.ones_like(density))


def along_z(field):
    return (jnp.roll(field, -1, 2) - jnp.roll(field, 1, 2)) * 0.5


def flux_parts(extended):
    middle = extended[1:-1, 1:-1]
    grad_x = (extended[2:, 1:-1] - extended[:-2, 1:-1]) * 0.5
    grad_y = (extended[1:-1, 2:] - extended[1:-1, :-2]) * 0.5
    grad_z = along_z(middle)
    sigma = grad_y * grad_y + grad_x * grad_x + grad_z * grad_z
    e_n, e_sigma = xc_parts(middle, sigma)
    return (e_n, 2.0 * e_sigma * grad_y, 2.0 * e_sigma * grad_x, 2.0 * e_sigma * grad_z)


def from_single(density):
    extended = padded(density, (("band", 1), ("dom", 0)), 1)
    e_n, flux_y, flux_x, flux_z = flux_parts(extended)
    outer = padded(jnp.stack([flux_y, flux_x]), (("band", 2), ("dom", 1)), 1)
    divergence = (
        outer[0, 1:-1, 2:] - outer[0, 1:-1, :-2] + (outer[1, 2:, 1:-1] - outer[1, :-2, 1:-1])
    ) * 0.5 + along_z(flux_z)
    return e_n - divergence


def shards(orbitals, occupation, core_density, proj_values, block_index, live_points):
    weights = occupation.astype(jnp.float32) * 0.001
    local_orbs, width_x, full_y, depth_z = orbitals.shape
    partial_value = jnp.zeros((width_x, full_y, depth_z), jnp.float32)
    for orbit in range(local_orbs):
        partial_value = partial_value + weights[orbit] * orbitals[orbit] * orbitals[orbit]
    flat = orbitals.reshape(local_orbs, width_x * full_y * depth_z)
    blocks, points = block_index.shape
    point_ids = lax.broadcasted_iota(jnp.int32, (blocks, points), 1)
    mask = (point_ids < live_points[:, None]).astype(jnp.float32)
    beta = proj_values * mask[:, None, :]
    picked = flat[:, block_index]
    coeff = jnp.einsum("obk,bpk->obp", picked, beta, precision=lax.Precision.HIGHEST)
    strength = jnp.einsum("o,obp->bp", weights, coeff * coeff, precision=lax.Precision.HIGHEST)
    at_points = jnp.einsum("bp,bpk->bk", strength, beta * beta, precision=lax.Precision.HIGHEST)
    augment = (
        jnp.zeros((width_x * full_y * depth_z,), jnp.float32)
        .at[block_index.reshape(-1)]
        .add(at_points.reshape(-1))
    )
    partial_value = partial_value + augment.reshape(width_x, full_y, depth_z)
    summed = lax.psum_scatter(partial_value, "band", scatter_dimension=1, tiled=True)
    density = summed + core_density
    potential = from_single(density)
    return potential


def solution(mesh):
    placed = (
        P("band", "dom", None, None),
        P("band"),
        P("dom", "band", None),
        P("dom", None, None),
        P("dom", None),
        P("dom"),
    )
    return jax.shard_map(
        shards, mesh=mesh, in_specs=placed, out_specs=P("dom", "band", None), check_vma=False
    )
```

profile of v0, /device:TPU:0, one launch (start us, length us, event | category | flops | bytes accessed | tf_op | source)
XLA Modules:
  0.0 365.3 jit_solution(11595524926307980335)
XLA Ops:
  6.5 0.7 fusion.41
  7.9 28.6 %copy.20 = f32[1,2,4096,512]{3,1,2,0:T(2,128)} copy(f32[1,2,4096,512]{3,2,1,0:T(8,128)} %bitcast.44) | data formatting | bytes 33554432
  36.6 91.3 %gather_fusion = f32[8192,2]{0,1:T(2,128)S(1)} fusion(f32[2,2097152]{1,0:T(2,128)} %bitcast.45, s32[8192]{0:T(1024)S(1)} %fusion.40), kind=kCustom, calls=%fused_computation | custom fusion | bytes 163840 | tf_op jit(solution)/shard_map/gather | solution.py:77
  129.8 46.9 %scatter_custom_fusion = f32[2097152]{0:T(1024)} fusion(s32[8192]{0:T(1024)S(1)} %bitcast.50, f32[8192]{0:T(1024)S(1)} %bitcast.51, f32[]{:T(128)} %constant.5.clone.1), kind=kCustom, calls=%fused_computation.12 | custom fusion | flops 8192 | bytes 8388612 | tf_op jit(solution)/shard_map/scatter-add | solution.py:84
  176.7 9.3 %reshape.62 = f32[8,512,512]{2,1,0:T(8,128)} reshape(f32[2097152]{0:T(1024)} %scatter_custom_fusion) | data formatting | bytes 16777216 | tf_op jit(solution)/shard_map/reshape | solution.py:86
  186.0 14.6 %fusion.1 = f32[8,512,512]{2,1,0:T(8,128)} fusion(f32[8,512,512]{2,1,0:T(8,128)} %reshape.62, f32[2,8,512,512]{3,2,1,0:T(8,128)} %param.6, f32[]{:T(128)} %bitcast.2, f32[]{:T(128)} %bitcast), kind=kLoop, calls=%fused_computation.5 | loop fusion | flops 12582912 | bytes 33554440 | tf_op jit(solution)/shard_map/add | solution.py:86
  200.6 81.4 %reduce-scatter.2.cloned.1.call-done = f32[8,128,512]{2,1,0:T(8,128)} async-done(((f32[8,512,512]{2,1,0:T(8,128)}), f32[8,128,512]{2,1,0:T(8,128)}) %reduce-scatter.2.cloned.1.call-update) | async-done | bytes 2097168 | tf_op jit(solution)/shard_map/reduce_scatter | solution.py:87
  282.0 2.7 add.57
  285.3 0.9 collective-permute-done
  286.2 3.4 collective-permute-done.1
  289.7 5.6 %collective-permute-start.2 = (f32[1,130,512]{2,1,0:T(8,128)S(1)}, f32[1,130,512]{2,1,0:T(8,128)S(1)}, u32[]{:S(2)}, u32[]{:S(2)}) collective-permute-start(f32[1,130,512]{2,1,0:T(8,128)S(1)} %get-tuple-element.12), channel_id=1, source_target_pairs={{1,0},{2,1},{3,2},{4,3},{5,4},{6,5},{7,6},{8,7},{9,8},{10,9},{11,1... | collective-permute-start | bytes 798728 | tf_op jit(solution)/shard_map/ppermute | solution.py:23
  295.3 0.7 fusion.46
  296.2 4.2 %collective-permute-done.2 = f32[1,130,512]{2,1,0:T(8,128)S(1)} collective-permute-done((f32[1,130,512]{2,1,0:T(8,128)S(1)}, f32[1,130,512]{2,1,0:T(8,128)S(1)}, u32[]{:S(2)}, u32[]{:S(2)}) %collective-permute-start.2) | collective-permute-done | bytes 266272 | tf_op jit(solution)/shard_map/ppermute | solution.py:23
  300.4 6.4 %collective-permute-done.3 = f32[1,130,512]{2,1,0:T(8,128)S(1)} collective-permute-done((f32[1,130,512]{2,1,0:T(8,128)S(1)}, f32[1,130,512]{2,1,0:T(8,128)S(1)}, u32[]{:S(2)}, u32[]{:S(2)}) %collective-permute-start.3) | collective-permute-done | bytes 266272 | tf_op jit(solution)/shard_map/ppermute | solution.py:21
  306.9 6.8 %multiply_bitcast_fusion = (f32[1,8,128,512]{3,2,1,0:T(8,128)S(1)}, f32[8,128,512]{2,1,0:T(8,128)S(1)}, f32[8,128,512]{2,1,0:T(8,128)S(1)}) fusion(f32[8,1,512]{2,1,0:T(1,128)S(1)} %collective-permute-done, f32[8,128,512]{2,1,0:T(8,128)S(1)} %add.57, f32[8,1,512]{2,1,0:T(1,128)S(1)} %collective-permute-done.1, f32[1,130,512]{2,1,0:T(8,128)S(1)} %collective-permute-done.3, ...), kind=kLoop, calls=%fused_computation.52 | loop fusion | flops 19922944 | bytes 13148160 | tf_op jit(solution)/shard_map/stack | solution.py:59
  313.7 1.2 multiply_bitcast_fusion.1
  316.4 3.6 collective-permute-done.5
  320.0 3.5 copy_dynamic-update-slice_fusion
  324.3 1.7 collective-permute-start.7
  326.0 0.8 fusion.45
  327.3 9.0 %collective-permute-done.6 = f32[2,1,130,512]{3,0,2,1:T(2,128)S(1)} collective-permute-done((f32[2,1,130,512]{3,0,2,1:T(2,128)S(1)}, f32[2,1,130,512]{3,0,2,1:T(2,128)S(1)}, u32[]{:S(2)}, u32[]{:S(2)}) %collective-permute-start.6) | collective-permute-done | bytes 532512 | tf_op jit(solution)/shard_map/ppermute | solution.py:23
  336.3 4.5 %collective-permute-done.7 = f32[2,1,130,512]{3,0,2,1:T(2,128)S(1)} collective-permute-done((f32[2,1,130,512]{3,0,2,1:T(2,128)S(1)}, f32[2,1,130,512]{3,0,2,1:T(2,128)S(1)}, u32[]{:S(2)}, u32[]{:S(2)}) %collective-permute-start.7) | collective-permute-done | bytes 532512 | tf_op jit(solution)/shard_map/ppermute | solution.py:21
  340.8 12.1 %fusion.12 = f32[1,8,128,512]{3,0,2,1:T(1,128)S(1)} fusion(f32[2,8,130,512]{3,0,2,1:T(2,128)S(1)} %copy_dynamic-update-slice_fusion.1, f32[2,1,130,512]{3,0,2,1:T(2,128)S(1)} %collective-permute-done.7, f32[2,1,130,512]{3,0,2,1:T(2,128)S(1)} %collective-permute-done.6, f32[1,8,128,512]{3,2,1,0:T(8,128)S(1)} %fusion.13), kind=kLoop, calls=%fused_computation.28 | loop fusion | flops 2097152 | bytes 9519104 | tf_op jit(solution)/shard_map/add | solution.py:61
  352.9 5.5 %fusion.5 = f32[8,128,512]{2,1,0:T(8,128)} fusion(f32[8,128,512]{2,1,0:T(8,128)S(1)} %add.57, f32[8,128,1]{2,1,0:T(8,128)S(1)} %get-tuple-element.17, f32[8,128,511]{2,1,0:T(8,128)S(1)} %get-tuple-element.19, f32[8,128,511]{2,1,0:T(8,128)S(1)} %get-tuple-element.18, f32[8,128,1]{2,1,0:T(8,128)S(1)} %get-tuple-element.16, f32[1,8,128,512]{3,0,2,1:T(1,128)S(1)} %fusion.12, ...), kind=kLoop, calls=%fused_computation.20 | loop fusion | flops 20971520 | bytes 12582912 | tf_op jit(solution)/shard_map/sub | solution.py:63
  (30 shorter events, 6.1 us)
Async XLA Ops:
  6.5 275.4 %reduce-scatter.2.cloned.1.call-start = ((), (), s32[]{:S(2)}) async-start(), calls=%async_computation.1 | async-start | bytes 10485760 | tf_op jit(solution)/shard_map/reduce_scatter | solution.py:87
  7.9 28.6 %copy-start.1 = (s32[64,128]{1,0:T(8,128)S(1)}, s32[64,128]{1,0:T(8,128)}, u32[]{:S(2)}) copy-start(s32[64,128]{1,0:T(8,128)} %param.10) | copy-start | bytes 98308
  36.5 92.0 %copy-start = (f32[64,8,128]{2,1,0:T(8,128)S(1)}, f32[64,8,128]{2,1,0:T(8,128)}, u32[]{:S(2)}) copy-start(f32[64,8,128]{2,1,0:T(8,128)} %param.9) | copy-start | bytes 786436
  284.7 1.5 collective-permute-start
  284.8 4.9 %collective-permute-start.1 = (f32[8,1,512]{2,1,0:T(1,128)S(1)}, f32[8,1,512]{2,1,0:T(1,128)S(1)}, u32[]{:S(2)}, u32[]{:S(2)}) collective-permute-start(f32[8,1,512]{2,1,0:T(1,128)S(1)} %get-tuple-element.24), channel_id=1, source_target_pairs={{0,32},{32,64},{64,96},{96,0},{1,33},{33,65},{65,97},{97,1},{2,34}... | collective-permute-start | bytes 49160 | tf_op jit(solution)/shard_map/ppermute | solution.py:21
  289.7 10.7 %collective-permute-start.2 = (f32[1,130,512]{2,1,0:T(8,128)S(1)}, f32[1,130,512]{2,1,0:T(8,128)S(1)}, u32[]{:S(2)}, u32[]{:S(2)}) collective-permute-start(f32[1,130,512]{2,1,0:T(8,128)S(1)} %get-tuple-element.12), channel_id=1, source_target_pairs={{1,0},{2,1},{3,2},{4,3},{5,4},{6,5},{7,6},{8,7},{9,8},{10,9},{11,1... | collective-permute-start | bytes 798728 | tf_op jit(solution)/shard_map/ppermute | solution.py:23
  295.3 11.6 %collective-permute-start.3 = (f32[1,130,512]{2,1,0:T(8,128)S(1)}, f32[1,130,512]{2,1,0:T(8,128)S(1)}, u32[]{:S(2)}, u32[]{:S(2)}) collective-permute-start(f32[1,130,512]{2,1,0:T(8,128)S(1)} %get-tuple-element.13), channel_id=1, source_target_pairs={{0,1},{1,2},{2,3},{3,4},{4,5},{5,6},{6,7},{7,8},{8,9},{9,10},{10,1... | collective-permute-start | bytes 798728 | tf_op jit(solution)/shard_map/ppermute | solution.py:21
  315.0 8.5 %collective-permute-start.4 = (f32[2,8,1,512]{3,2,1,0:T(1,128)S(1)}, f32[2,8,1,512]{3,2,1,0:T(1,128)S(1)}, u32[]{:S(2)}, u32[]{:S(2)}) collective-permute-start(f32[2,8,1,512]{3,2,1,0:T(1,128)S(1)} %get-tuple-element.10), channel_id=1, source_target_pairs={{32,0},{64,32},{96,64},{0,96},{33,1},{65,33},{97,65},{1,97},{34,2}... | collective-permute-start | bytes 98312 | tf_op jit(solution)/shard_map/ppermute | solution.py:23
  315.1 4.9 %collective-permute-start.5 = (f32[2,8,1,512]{3,2,1,0:T(1,128)S(1)}, f32[2,8,1,512]{3,2,1,0:T(1,128)S(1)}, u32[]{:S(2)}, u32[]{:S(2)}) collective-permute-start(f32[2,8,1,512]{3,2,1,0:T(1,128)S(1)} %get-tuple-element.11), channel_id=1, source_target_pairs={{0,32},{32,64},{64,96},{96,0},{1,33},{33,65},{65,97},{97,1},{2,34}... | collective-permute-start | bytes 98312 | tf_op jit(solution)/shard_map/ppermute | solution.py:21
  323.9 12.4 %collective-permute-start.6 = (f32[2,1,130,512]{3,0,2,1:T(2,128)S(1)}, f32[2,1,130,512]{3,0,2,1:T(2,128)S(1)}, u32[]{:S(2)}, u32[]{:S(2)}) collective-permute-start(f32[2,1,130,512]{3,0,2,1:T(2,128)S(1)} %get-tuple-element.8), channel_id=1, source_target_pairs={{1,0},{2,1},{3,2},{4,3},{5,4},{6,5},{7,6},{8,7},{9,8},{10,9},{11,1... | collective-permute-start | bytes 1597448 | tf_op jit(solution)/shard_map/ppermute | solution.py:23
  324.3 16.5 %collective-permute-start.7 = (f32[2,1,130,512]{3,0,2,1:T(2,128)S(1)}, f32[2,1,130,512]{3,0,2,1:T(2,128)S(1)}, u32[]{:S(2)}, u32[]{:S(2)}) collective-permute-start(f32[2,1,130,512]{3,0,2,1:T(2,128)S(1)} %get-tuple-element.9), channel_id=1, source_target_pairs={{0,1},{1,2},{2,3},{3,4},{4,5},{5,6},{6,7},{7,8},{8,9},{9,10},{10,1... | collective-permute-start | bytes 1597448 | tf_op jit(solution)/shard_map/ppermute | solution.py:21
Sparse Core Ops, SparseCore 0:
  200.7 81.2 reduce-scatter.1
where the time goes:
time: 367 us; the launch traced here: 365 us
  local copies, waits for them, and re-layouts  136 us (37%)
  waiting for transfers between devices  114 us (31%)
  other arithmetic  92.5 us (25%)
  between operations  13.6 us (4%)
  starting transfers between devices  8.8 us (2%)
    gather x1, local copies, waits for them, and re-layouts, shards(): picked = flat[:, block_index]  91.3 us
    reduce_scatter x1, waiting for transfers between devices, shards(): lax.psum_scatter(partial_value, 'band', scatter_dimension=1, tiled=True)  81.4 us
    scatter-add x1, other arithmetic, shards(): augment = jnp.zeros((width_x * full_y * depth_z,), jnp.float32).at[block_...  46.9 us
    unnamed x8, local copies, waits for them, and re-layouts  32.1 us
    ppermute x4, waiting for transfers between devices, padded(): lax.ppermute(tail, axis, [(i, (i + 1) % count) for i in range(count)])  18 us
    add x1, other arithmetic, shards(): partial_value = partial_value + augment.reshape(width_x, full_y, depth_z)  14.6 us
    ppermute x4, waiting for transfers between devices, padded(): lax.ppermute(head, axis, [((i + 1) % count, i) for i in range(count)])  14.2 us
    add x1, other arithmetic, from_single(): outer[0, 1:-1, 2:] - outer[0, 1:-1, :-2]  12.1 us
  transfers between devices with their start and end apart: 9, of which 8 were waited for; matrix products, arithmetic and copies ran while one was open for 2% of the time, Pallas kernels for 0%

commit v1 on v0

v1 whole, which is shorter than its diff:
```python
import functools
import math

import jax
import jax.numpy as jnp
from jax import lax
from jax.experimental import pallas as pl
from jax.experimental.pallas import tpu as pltpu
from jax.sharding import PartitionSpec as P

f32 = jnp.float32
bf16 = jnp.bfloat16
i32 = jnp.int32

coef_a = 0.75 * (3.0 / math.pi) ** (1.0 / 3.0)
kappa_val = 0.804
mu_val = 0.2195149727645171
s_scale = 4.0 * (3.0 * math.pi**2) ** (2.0 / 3.0)

MIB = 2**20
GROUP = 264
LOW = 256
HIGH = 260
ACC_ROWS = 16 * GROUP
N_ACC = 8
NT = (((1,), (1,)), ((), ()))
VM = pl.BlockSpec(memory_space=pltpu.VMEM)
SM = pl.BlockSpec(memory_space=pltpu.SMEM)
ANY = pl.BlockSpec(memory_space=pl.ANY)


def params(mib):
    return pltpu.CompilerParams(vmem_limit_bytes=mib * MIB)


def valence_kernel(place, weights, orb_ref, core_ref, keep_ref, send_ref):
    band = place[0]
    parity = place[1]
    z_hi = place[2]
    w0 = weights[0]
    w1 = weights[1]

    def squares(row, count):
        a = orb_ref[0, 0, pl.ds(row, count), :]
        b = orb_ref[1, 0, pl.ds(row, count), :]
        return w0 * a * a + w1 * b * b

    def plane(i):
        for near in range(2):
            for ref, par in ((keep_ref, parity), (send_ref, 1 - parity)):
                q = 2 * jnp.where(near == 1, z_hi, 1 - z_hi) + par
                for part in range(2):
                    row = pl.multiple_of(q * 128 + 64 * part, 64)
                    own = jnp.where(q == band, 1.0, 0.0)
                    ref[near, 0, pl.ds(128 * i + 64 * part, 64), :] = (
                        squares(row, 64) + own * core_ref[0, 64 * part : 64 * part + 64, :]
                    )
                q_low = (q + 3) % 4
                own = jnp.where(q_low == band, 1.0, 0.0)
                tile = squares(pl.multiple_of(q_low * 128 + 120, 8), 8) + own * core_ref[0, 120:128, :]
                ref[near, 0, pl.ds(LOW + 2 * i, 2), :] = tile[6:8]
                q_high = (q + 1) % 4
                own = jnp.where(q_high == band, 1.0, 0.0)
                tile = squares(pl.multiple_of(q_high * 128, 8), 8) + own * core_ref[0, 0:8, :]
                ref[near, 0, pl.ds(HIGH + 2 * i, 2), :] = tile[0:2]

    for i in range(2):
        pl.when(pl.program_id(0) % 2 == i)(functools.partial(plane, i))


def valence(place, weights, orbitals, core, planes, name):
    first, second = planes

    def plane_of(s):
        return jnp.where(s < 2, first + s, second + s - 2)

    out = jax.ShapeDtypeStruct((2, 2, GROUP, 512), f32)
    return pl.pallas_call(
        valence_kernel,
        grid=(4,),
        in_specs=[
            SM,
            SM,
            pl.BlockSpec((2, 1, 512, 512), lambda s: (0, plane_of(s), 0, 0)),
            pl.BlockSpec((1, 128, 512), lambda s: (plane_of(s), 0, 0)),
        ],
        out_specs=[pl.BlockSpec((2, 1, GROUP, 512), lambda s: (0, s // 2, 0, 0))] * 2,
        out_shape=[out, out],
        compiler_params=params(24),
        cost_estimate=pl.CostEstimate(flops=8 * MIB, bytes_accessed=13 * MIB, transcendentals=0),
        name=name,
    )(place, weights, orbitals, core)


def gather_kernel(weights, rows, lanes, beta, orb, w_ref, buf, picked, sem):
    copies = []
    for o in range(2):
        for x in range(8):
            for c in range(4):
                copy = pltpu.make_async_copy(
                    orb.at[o, x, :, :, pl.ds(128 * c, 128)],
                    buf.at[pl.ds((x * 4 + c) * 64, 64), o],
                    sem.at[o * 32 + x * 4 + c],
                )
                copy.start()
                copies.append(copy)
    for copy in copies:
        copy.wait()
    flat = buf.reshape(32768, 128)
    sub = lax.broadcasted_iota(i32, (128, 128), 0)
    eye = sub == lax.broadcasted_iota(i32, (128, 128), 1)
    lane_ids = lax.broadcasted_iota(i32, (8, 128), 1)
    w0 = weights[0]
    w1 = weights[1]

    def block(b, total):
        for k in range(128):
            r = rows[b, k]
            picked[pl.ds(k, 1), :] = flat[pl.ds(r, 1), :]
            picked[pl.ds(128 + k, 1), :] = flat[pl.ds(r + 8, 1), :]
        hot = jnp.where(lanes[pl.ds(b, 1), :] == sub, 1.0, 0.0).astype(bf16)
        g = picked[...]
        g1 = g.astype(bf16)
        rest = g - g1.astype(f32)
        g2 = rest.astype(bf16)
        g3 = (rest - g2.astype(f32)).astype(bf16)
        t = (
            jnp.dot(g1, hot, preferred_element_type=f32)
            + jnp.dot(g2, hot, preferred_element_type=f32)
            + jnp.dot(g3, hot, preferred_element_type=f32)
        )
        be = beta[b]
        p0 = jnp.sum(jnp.where(eye, t[:128], 0.0), axis=0, keepdims=True)
        p1 = jnp.sum(jnp.where(eye, t[128:], 0.0), axis=0, keepdims=True)
        c0 = jnp.sum(be * p0, axis=1, keepdims=True)
        c1 = jnp.sum(be * p1, axis=1, keepdims=True)
        return jnp.where(lane_ids == b, w0 * c0 * c0 + w1 * c1 * c1, total)

    w_ref[...] = lax.fori_loop(0, 64, block, jnp.zeros((8, 128), f32))


def gather(weights, rows, lanes, beta, orbitals):
    return pl.pallas_call(
        gather_kernel,
        in_specs=[SM, SM, VM, VM, ANY],
        out_specs=VM,
        out_shape=jax.ShapeDtypeStruct((8, 128), f32),
        scratch_shapes=[
            pltpu.VMEM((2048, 2, 8, 128), f32),
            pltpu.VMEM((256, 128), f32),
            pltpu.SemaphoreType.DMA((64,)),
        ],
        compiler_params=params(24),
        cost_estimate=pl.CostEstimate(flops=100 * MIB, bytes_accessed=80 * MIB, transcendentals=0),
        name="gather_points",
    )(weights, rows, lanes, beta, orbitals.reshape(2, 8, 64, 8, 512))


def scatter_kernel(
    rows, lanes, beta, s0, s1, s2, s3, keep, recv, far, d0_ref, d3_ref, aug_ref, spread, *accs
):
    for acc in accs:
        acc[...] = jnp.zeros_like(acc)
    strengths = (s0[...] + s1[...]) + (s2[...] + s3[...])
    sub = lax.broadcasted_iota(i32, (128, 128), 0)
    eye = sub == lax.broadcasted_iota(i32, (128, 128), 1)
    lane_ids = lax.broadcasted_iota(i32, (8, 128), 1)

    def block(b, _):
        be = beta[b]
        w = jnp.sum(jnp.where(lane_ids == b, strengths, 0.0), axis=1, keepdims=True)
        at = jnp.sum(w * be * be, axis=0, keepdims=True)
        a1 = at.astype(bf16).astype(f32)
        rest = at - a1
        a2 = rest.astype(bf16).astype(f32)
        a3 = rest - a2
        hot = jnp.where(lanes[pl.ds(b, 1), :] == sub, 1.0, 0.0).astype(bf16)
        total = None
        for part in (a1, a2, a3):
            diag = jnp.where(eye, part, 0.0).astype(bf16)
            term = lax.dot_general(diag, hot, NT, preferred_element_type=f32)
            total = term if total is None else total + term
        spread[...] = total
        for k in range(0, 128, N_ACC):
            at_rows = [rows[b, k + j] for j in range(N_ACC)]
            old = [accs[j][pl.ds(at_rows[j], 1), :] for j in range(N_ACC)]
            for j in range(N_ACC):
                accs[j][pl.ds(at_rows[j], 1), :] = old[j] + spread[pl.ds(k + j, 1), :]
        return 0

    lax.fori_loop(0, 64, block, 0)

    def summed(g, c):
        piece = pl.ds((g * 4 + c) * GROUP, GROUP)
        total = accs[0][piece, :]
        for acc in accs[1:]:
            total = total + acc[piece, :]
        return total

    for at, g, ref in ((0, 0, d0_ref), (1, 3, d3_ref)):
        for c in range(4):
            cols = slice(128 * c, 128 * c + 128)
            ref[:, cols] = (keep[0, at, :, cols] + recv[0, at, :, cols]) + far[at, :, cols] + summed(g, c)
    for at, g in ((0, 1), (1, 2)):
        for c in range(4):
            aug_ref[at, :, 128 * c : 128 * c + 128] = summed(g, c)


def scatter(rows, lanes, beta, strengths, keep, recv, far):
    group = jax.ShapeDtypeStruct((GROUP, 512), f32)
    near = pl.BlockSpec((1, 2, GROUP, 512), lambda s: (1, 0, 0, 0))
    whole2 = lambda *shape: pl.BlockSpec(shape, lambda s: (0,) * len(shape))
    return pl.pallas_call(
        scatter_kernel,
        grid=(1,),
        in_specs=[
            SM,
            whole2(64, 128),
            whole2(64, 8, 128),
            *[whole2(8, 128)] * 4,
            near,
            near,
            whole2(2, GROUP, 512),
        ],
        out_specs=[whole2(GROUP, 512), whole2(GROUP, 512), whole2(2, GROUP, 512)],
        out_shape=[group, group, jax.ShapeDtypeStruct((2, GROUP, 512), f32)],
        scratch_shapes=[pltpu.VMEM((128, 128), f32)] + [pltpu.VMEM((ACC_ROWS + 8, 128), f32)] * N_ACC,
        compiler_params=params(44),
        cost_estimate=pl.CostEstimate(flops=100 * MIB, bytes_accessed=80 * MIB, transcendentals=0),
        name="scatter_points",
    )(rows, lanes, beta, *strengths, keep, recv, far)


def place_group(dens, plane, group, lead=None):
    for i in range(2):
        dens[plane + i, 16:144, :] = group[pl.ds(128 * i, 128), :]
        dens[plane + i, 14:16, :] = group[pl.ds(LOW + 2 * i, 2), :]
        dens[plane + i, 144:146, :] = group[pl.ds(HIGH + 2 * i, 2), :]


def local_parts(dens, x, row, count):
    mid = dens[x, pl.ds(row, count), :]
    gy = (dens[x, pl.ds(row + 1, count), :] - dens[x, pl.ds(row - 1, count), :]) * 0.5
    gx = (dens[x + 1, pl.ds(row, count), :] - dens[x - 1, pl.ds(row, count), :]) * 0.5
    gz = (pltpu.roll(mid, 511, 1) - pltpu.roll(mid, 1, 1)) * 0.5
    sigma = gy * gy + gx * gx + gz * gz
    logs = jnp.log(mid)
    cube = jnp.exp(logs * (1.0 / 3.0))
    inv_four = jnp.exp(logs * (-4.0 / 3.0))
    reduced = sigma * (inv_four * inv_four) * (1.0 / s_scale)
    inv = 1.0 / (1.0 + (mu_val / kappa_val) * reduced)
    slope = mu_val * inv * inv
    factor = (1.0 + kappa_val) - kappa_val * inv
    e_n = (-4.0 / 3.0 * coef_a) * cube * (factor - 2.0 * reduced * slope)
    twice = (-2.0 * coef_a / s_scale) * inv_four * slope
    return e_n, twice * gy, twice * gx, twice * gz


STRIP = 16


def full_plane(dens, x, flux_y, put):
    for row in (8, 144):
        flux_y[pl.ds(row, 8), :] = local_parts(dens, x, row, 8)[1]
    for row in range(16, 144, STRIP):
        e_n, fy, fx, fz = local_parts(dens, x, row, STRIP)
        flux_y[pl.ds(row, STRIP), :] = fy
        put(row - 16, e_n - (pltpu.roll(fz, 511, 1) - pltpu.roll(fz, 1, 1)) * 0.5, fx)


def minus_y(flux_y, row):
    up = flux_y[pl.ds(row + 17, STRIP), :]
    down = flux_y[pl.ds(row + 15, STRIP), :]
    return (up - down) * 0.5


def inner_kernel(d0, d3, keep, recv, far, aug, pot_ref, low_ref, high_ref, dens, flux_x, flux_y):
    place_group(dens, 0, d0)
    place_group(dens, 6, d3)
    for g in range(2):
        total = (keep[0, g] + recv[0, g]) + far[g] + aug[g]
        for i in range(2):
            dens[2 + 2 * g + i, 16:144, :] = total[128 * i : 128 * i + 128]
            dens[2 + 2 * g + i, 14:16, :] = total[LOW + 2 * i : LOW + 2 * i + 2]
            dens[2 + 2 * g + i, 144:146, :] = total[HIGH + 2 * i : HIGH + 2 * i + 2]

    def plane(x, _):
        def put(row, value, fx):
            pot_ref[x, pl.ds(row, STRIP), :] = value
            flux_x[x, pl.ds(row, STRIP), :] = fx

        full_plane(dens, x, flux_y, put)
        for row in range(0, 128, STRIP):
            here = pl.ds(row, STRIP)
            pot_ref[x, here, :] = pot_ref[x, here, :] - minus_y(flux_y, row)
        return 0

    lax.fori_loop(1, 7, plane, 0)

    def across(x, _):
        for row in range(0, 128, STRIP):
            here = pl.ds(row, STRIP)
            pot_ref[x, here, :] = (
                pot_ref[x, here, :] - (flux_x[x + 1, here, :] - flux_x[x - 1, here, :]) * 0.5
            )
        return 0

    lax.fori_loop(2, 6, across, 0)
    pot_ref[1] = pot_ref[1] - flux_x[2] * 0.5
    pot_ref[6] = pot_ref[6] + flux_x[5] * 0.5
    pot_ref[0] = jnp.zeros((128, 512), f32)
    pot_ref[7] = jnp.zeros((128, 512), f32)
    low_ref[...] = flux_x[1]
    high_ref[...] = flux_x[6]


def inner(d0, d3, keep, recv, far, aug):
    near = pl.BlockSpec((1, 2, GROUP, 512), lambda s: (1, 0, 0, 0))
    whole2 = lambda *shape: pl.BlockSpec(shape, lambda s: (0,) * len(shape))
    plane = jax.ShapeDtypeStruct((128, 512), f32)
    return pl.pallas_call(
        inner_kernel,
        grid=(1,),
        in_specs=[whole2(GROUP, 512)] * 2 + [near, near] + [whole2(2, GROUP, 512)] * 2,
        out_specs=[whole2(8, 128, 512), whole2(128, 512), whole2(128, 512)],
        out_shape=[jax.ShapeDtypeStruct((8, 128, 512), f32), plane, plane],
        scratch_shapes=[
            pltpu.VMEM((8, 160, 512), f32),
            pltpu.VMEM((8, 128, 512), f32),
            pltpu.VMEM((160, 512), f32),
        ],
        compiler_params=params(40),
        cost_estimate=pl.CostEstimate(flops=100 * MIB, bytes_accessed=30 * MIB, transcendentals=0),
        name="inner_planes",
    )(d0, d3, keep, recv, far, aug)


def outer_kernel(below, d0, d3, above, old, low, high, pot_ref, dens, flux_x, flux_y):
    place_group(dens, 0, below)
    place_group(dens, 2, d0)
    place_group(dens, 4, d3)
    place_group(dens, 6, above)
    for row in range(0, 128, STRIP):
        flux_x[0, pl.ds(row, STRIP), :] = local_parts(dens, 1, row + 16, STRIP)[2]
        flux_x[1, pl.ds(row, STRIP), :] = local_parts(dens, 6, row + 16, STRIP)[2]

    for end, x, edge, inside in ((0, 2, 0, 1), (1, 5, 3, 2)):

        def put(row, value, fx):
            here = pl.ds(row, STRIP)
            pot_ref[edge, here, :] = value
            if end == 0:
                pot_ref[inside, here, :] = old[1, here, :] + 0.5 * fx
            else:
                pot_ref[inside, here, :] = old[2, here, :] - 0.5 * fx

        full_plane(dens, x, flux_y, put)
        for row in range(0, 128, STRIP):
            here = pl.ds(row, STRIP)
            if end == 0:
                across = (low[here, :] - flux_x[0, here, :]) * 0.5
            else:
                across = (flux_x[1, here, :] - high[here, :]) * 0.5
            pot_ref[edge, here, :] = pot_ref[edge, here, :] - minus_y(flux_y, row) - across


def outer_body(below, d0, d3, above, old_ref, low, high, pot_ref, dens, flux_x, flux_y, old, new, sem):
    ins = [
        pltpu.make_async_copy(old_ref.at[pl.ds(0, 2)], old.at[pl.ds(0, 2)], sem.at[0]),
        pltpu.make_async_copy(old_ref.at[pl.ds(6, 2)], old.at[pl.ds(2, 2)], sem.at[1]),
    ]
    for copy in ins:
        copy.start()
    for copy in ins:
        copy.wait()
    outer_kernel(below, d0, d3, above, old, low, high, new, dens, flux_x, flux_y)
    outs = [
        pltpu.make_async_copy(new.at[pl.ds(0, 2)], pot_ref.at[pl.ds(0, 2)], sem.at[2]),
        pltpu.make_async_copy(new.at[pl.ds(2, 2)], pot_ref.at[pl.ds(6, 2)], sem.at[3]),
    ]
    for copy in outs:
        copy.start()
    for copy in outs:
        copy.wait()


def outer(below, d0, d3, above, old, low, high):
    return pl.pallas_call(
        outer_body,
        in_specs=[VM, VM, VM, VM, ANY, VM, VM],
        out_specs=ANY,
        out_shape=jax.ShapeDtypeStruct((8, 128, 512), f32),
        input_output_aliases={4: 0},
        scratch_shapes=[
            pltpu.VMEM((8, 160, 512), f32),
            pltpu.VMEM((2, 128, 512), f32),
            pltpu.VMEM((160, 512), f32),
            pltpu.VMEM((4, 128, 512), f32),
            pltpu.VMEM((4, 128, 512), f32),
            pltpu.SemaphoreType.DMA((4,)),
        ],
        compiler_params=params(40),
        cost_estimate=pl.CostEstimate(flops=100 * MIB, bytes_accessed=30 * MIB, transcendentals=0),
        name="outer_planes",
    )(below, d0, d3, above, old, low, high)


def shards(orbitals, occupation, core_density, proj_values, block_index, live_points):
    band = lax.axis_index("band")
    place = jnp.stack([band, band % 2, band // 2]).astype(i32)
    weights = occupation.astype(f32) * 0.001

    swap_pairs = [(0, 1), (1, 0), (2, 3), (3, 2)]
    far_pairs = [(0, 2), (2, 0), (1, 3), (3, 1)]

    keep_a, send_a = valence(place, weights, orbitals, core_density, (0, 6), "valence_outer")
    recv_a = lax.ppermute(send_a, "band", swap_pairs)
    keep_b, send_b = valence(place, weights, orbitals, core_density, (2, 4), "valence_inner")
    recv_b = lax.ppermute(send_b, "band", swap_pairs)
    far_a = lax.ppermute(keep_a[0] + recv_a[0], "band", far_pairs)
    far_b = lax.ppermute(keep_b[0] + recv_b[0], "band", far_pairs)

    point_ids = lax.broadcasted_iota(i32, block_index.shape, 1)
    beta = proj_values * (point_ids < live_points[:, None]).astype(f32)[:, None, :]
    x = block_index >> 18
    y = (block_index >> 9) & 511
    c = (block_index >> 7) & 3
    lanes = block_index & 127
    from_rows = ((x * 4 + c) * 64 + (y >> 3)) * 16 + (y & 7)
    own = (y - 128 * band) & 511
    pair = (x & 1) * 2
    inside = jnp.where(
        own < 128,
        (x & 1) * 128 + own,
        jnp.where(own >= 510, LOW + pair + own - 510, HIGH + pair + own - 128),
    )
    into_rows = jnp.where(
        (own < 130) | (own >= 510), ((x >> 1) * 4 + c) * GROUP + inside, ACC_ROWS
    )

    mine = gather(weights, from_rows, lanes, beta, orbitals)
    strengths = [mine] + [
        lax.ppermute(mine, "band", [(i, (i + step) % 4) for i in range(4)]) for step in (1, 2, 3)
    ]
    d0, d3, aug = scatter(into_rows, lanes, beta, strengths, keep_a, recv_a, far_a)
    above = lax.ppermute(d0, "dom", [((i + 1) % 32, i) for i in range(32)])
    below = lax.ppermute(d3, "dom", [(i, (i + 1) % 32) for i in range(32)])
    part, low, high = inner(d0, d3, keep_b, recv_b, far_b, aug)
    return outer(below, d0, d3, above, part, low, high)


def solution(mesh):
    placed = (
        P("band", "dom", None, None),
        P("band"),
        P("dom", "band", None),
        P("dom", None, None),
        P("dom", None),
        P("dom"),
    )
    return jax.shard_map(
        shards, mesh=mesh, in_specs=placed, out_specs=P("dom", "band", None), check_vma=False
    )
```

time: 367 us -> 123 us (0.34)
  local copies, waits for them, and re-layouts: 136 us -> 14.6 us
  waiting for transfers between devices: 114 us -> 5.54 us
  other arithmetic: 92.5 us -> 4.17 us
  Pallas kernels: 0 us -> 79.1 us
  between operations: 13.6 us -> 0.26 us
  starting transfers between devices: 8.8 us -> 17.5 us
    gather x1 -> x0, local copies, waits for them, and re-layouts: 91.3 us -> none  [shards(): picked = flat[:, block_index]]
    reduce_scatter x1 -> x0, waiting for transfers between devices: 81.4 us -> none  [shards(): lax.psum_scatter(partial_value, 'band', scatter_dimension=1, tiled=True)]
    pallas_call x0 -> x6, Pallas kernels: none -> 79.1 us  [the longest x1 32.6 us: gather(): pl.pallas_call(gather_kernel, in_specs=[SM, SM, VM, VM, ANY], out_specs=V...]
    scatter-add x1 -> x0, other arithmetic: 46.9 us -> none  [shards(): augment = jnp.zeros((width_x * full_y * depth_z,), jnp.float32).at[block_...]
    ppermute x8 -> x9, waiting for transfers between devices: 32.2 us -> 5.54 us  [the longest x1 3.46 us: shards(): below = lax.ppermute(d3, 'dom', [(i, (i + 1) % 32) for i in range(32)])]
    add x3, other arithmetic: 29.3 us -> 3.34 us  [the longest x1 1.34 us: shards(): far_a = lax.ppermute(keep_a[0] + recv_a[0], 'band', far_pairs)]
    unnamed x8 -> x22, local copies, waits for them, and re-layouts: 32.1 us -> 14.6 us
    reshape x1 -> x0, local copies, waits for them, and re-layouts: 9.33 us -> none  [shards(): partial_value = partial_value + augment.reshape(width_x, full_y, depth_z)]
  transfers between devices with their start and end apart: 9 -> 9, of which waited for: 8 -> 4; matrix products, arithmetic and copies ran while one was open for 2% -> 3% of each run, Pallas kernels for 0% -> 59%
where the time goes in v1:
time: 123 us; the launch traced here: 121 us
  Pallas kernels  79.1 us (64%)
  starting transfers between devices  17.5 us (14%)
  local copies, waits for them, and re-layouts  14.6 us (12%)
  waiting for transfers between devices  5.54 us (5%)
  other arithmetic  4.17 us (3%)
    pallas_call x1, Pallas kernels, gather(): pl.pallas_call(gather_kernel, in_specs=[SM, SM, VM, VM, ANY], out_specs=V...  32.6 us
    pallas_call x1, Pallas kernels, scatter(): pl.pallas_call(scatter_kernel, grid=(1,), in_specs=[SM, whole2(64, 128),...  26.9 us
    unnamed x22, local copies, waits for them, and re-layouts  14.6 us
    pallas_call x1, Pallas kernels, inner(): pl.pallas_call(inner_kernel, grid=(1,), in_specs=[whole2(GROUP, 512)] * 2...  8.77 us
    pallas_call x2, Pallas kernels, valence(): pl.pallas_call(valence_kernel, grid=(4,), in_specs=[SM, SM, pl.BlockSpec(...  5.89 us
    pallas_call x1, Pallas kernels, outer(): pl.pallas_call(outer_body, in_specs=[VM, VM, VM, VM, ANY, VM, VM], out_sp...  4.93 us
    ppermute x3, starting transfers between devices, shards(): lax.ppermute(mine, 'band', [(i, (i + step) % 4) for i in range(4)])  4.77 us
    ppermute x1, starting transfers between devices, shards(): above = lax.ppermute(d0, 'dom', [((i + 1) % 32, i) for i in range(32)])  4.74 us
  transfers between devices with their start and end apart: 9, of which 4 were waited for; matrix products, arithmetic and copies ran while one was open for 3% of the time, Pallas kernels for 59%

profile of v1, /device:TPU:0, one launch (start us, length us, event | category | flops | bytes accessed | tf_op | source)
XLA Modules:
  0.0 121.1 jit_solution(11499082698520583175)
XLA Ops:
  0.0 0.7 convert_multiply_fusion.weights
  0.7 5.8 %copy-done = f32[2,8,512,512]{3,2,1,0:T(8,128)S(1)} copy-done((f32[2,8,512,512]{3,2,1,0:T(8,128)S(1)}, f32[2,8,512,512]{3,2,1,0:T(8,128)}, u32[]{:S(2)}) %copy-start) | copy-done | bytes 16777240
  6.5 1.6 %copy-done.2 = f32[8,128,512]{2,1,0:T(8,128)S(1)} copy-done((f32[8,128,512]{2,1,0:T(8,128)S(1)}, f32[8,128,512]{2,1,0:T(8,128)}, u32[]{:S(2)}) %copy-start.2) | copy-done | bytes 2097176
  8.1 2.9 %valence_outer.1 = (f32[2,2,264,512]{3,2,1,0:T(8,128)S(1)}, f32[2,2,264,512]{3,2,1,0:T(8,128)S(1)}) custom-call(s32[3]{0:T(128)S(1)} %pad_add_fusion.place, f32[2]{0:T(128)S(1)} %convert_multiply_fusion.weights, f32[2,8,512,512]{3,2,1,0:T(8,128)S(1)} %copy-done, f32[8,128,512]{2,1,0:T(8,128)S(1)} %copy-done.2), custom_call_target="tpu_custom_call" | custom-call | flops 8388608 | bytes 13631488 | tf_op jit(solution)/shard_map/valence_outer/pallas_call | solution.py:78
  11.1 3.0 %valence_inner.1 = (f32[2,2,264,512]{3,2,1,0:T(8,128)S(1)}, f32[2,2,264,512]{3,2,1,0:T(8,128)S(1)}) custom-call(s32[3]{0:T(128)S(1)} %pad_add_fusion.place, f32[2]{0:T(128)S(1)} %convert_multiply_fusion.weights, f32[2,8,512,512]{3,2,1,0:T(8,128)S(1)} %copy-done, f32[8,128,512]{2,1,0:T(8,128)S(1)} %copy-done.2), custom_call_target="tpu_custom_call" | custom-call | flops 8388608 | bytes 13631488 | tf_op jit(solution)/shard_map/valence_inner/pallas_call | solution.py:78
  14.1 0.5 collective-permute-start.7
  14.6 0.7 collective-permute-done.3.recv
  15.4 1.3 %fusion.1 = f32[2,264,512]{2,1,0:T(8,128)} fusion(f32[2,2,264,512]{3,2,1,0:T(8,128)S(1)} %collective-permute-done.3.recv, f32[2,2,264,512]{3,2,1,0:T(8,128)S(1)} %get-tuple-element.15.keep), kind=kLoop, calls=%fused_computation.3 | loop fusion | flops 270336 | bytes 3244032 | tf_op jit(solution)/shard_map/add | solution.py:420
  16.7 4.0 %collective-permute-start.4 = (f32[2,264,512]{2,1,0:T(8,128)}, f32[2,264,512]{2,1,0:T(8,128)S(1)}, u32[]{:S(2)}, u32[]{:S(2)}) collective-permute-start(f32[2,264,512]{2,1,0:T(8,128)} %fusion.1), channel_id=1, source_target_pairs={{0,64},{64,0},{32,96},{96,32},{1,65},{65,1},{33,97},{97,33},{2,66}... | collective-permute-start | bytes 3244040 | tf_op jit(solution)/shard_map/ppermute | solution.py:420
  20.7 1.2 fusion
  21.9 1.4 %copy-done.3 = f32[2,2,264,512]{3,2,1,0:T(8,128)} copy-done((f32[2,2,264,512]{3,2,1,0:T(8,128)}, f32[2,2,264,512]{3,2,1,0:T(8,128)S(1)}, u32[]{:S(2)}) %copy-start.3) | copy-done | bytes 2162712
  23.3 1.8 %collective-permute-start.8 = (f32[2,264,512]{2,1,0:T(8,128)}, f32[2,264,512]{2,1,0:T(8,128)}, u32[]{:S(2)}, u32[]{:S(2)}) collective-permute-start(f32[2,264,512]{2,1,0:T(8,128)} %fusion), channel_id=1, source_target_pairs={{0,64},{64,0},{32,96},{96,32},{1,65},{65,1},{33,97},{97,33},{2,66}... | collective-permute-start | bytes 3244040 | tf_op jit(solution)/shard_map/ppermute | solution.py:421
  25.2 0.8 and_add_fusion
  26.0 5.8 %copy-done.1 = f32[2,8,512,512]{3,2,1,0:T(8,128)S(1)} copy-done((f32[2,8,512,512]{3,2,1,0:T(8,128)S(1)}, f32[2,8,512,512]{3,2,1,0:T(8,128)}, u32[]{:S(2)}) %copy-start.1) | copy-done | bytes 16777240
  31.8 32.6 %gather_points.1.s0 = f32[8,128]{1,0:T(8,128)S(1)} custom-call(f32[2]{0:T(128)S(1)} %convert_multiply_fusion.weights, s32[64,128]{1,0:T(8,128)S(1)} %get-tuple-element.25.rows, s32[64,128]{1,0:T(8,128)S(1)} %get-tuple-element.27.lanes, f32[64,8,128]{2,1,0:T(8,128)S(1)} %broadcast_multiply_fusion.beta, f32[2,8,64,8,512]{4,3,2,1,0:T(8,128)S(1)} %bitcast.8), custom_call_target="tpu_custom_call" | custom-call | flops 104857600 | bytes 83886080 | tf_op jit(solution)/shard_map/gather_points/pallas_call | solution.py:143
  64.5 1.7 %collective-permute-start.1 = (f32[8,128]{1,0:T(8,128)S(1)}, f32[8,128]{1,0:T(8,128)S(1)}, u32[]{:S(2)}, u32[]{:S(2)}) collective-permute-start(f32[8,128]{1,0:T(8,128)S(1)} %gather_points.1.s0), channel_id=1, source_target_pairs={{0,64},{32,96},{64,0},{96,32},{1,65},{33,97},{65,1},{97,33},{2,66}... | collective-permute-start | bytes 12296 | tf_op jit(solution)/shard_map/ppermute | solution.py:443
  66.3 2.9 %collective-permute-start.2 = (f32[8,128]{1,0:T(8,128)S(1)}, f32[8,128]{1,0:T(8,128)S(1)}, u32[]{:S(2)}, u32[]{:S(2)}) collective-permute-start(f32[8,128]{1,0:T(8,128)S(1)} %gather_points.1.s0), channel_id=1, source_target_pairs={{0,96},{32,0},{64,32},{96,64},{1,97},{33,1},{65,33},{97,65},{2,98}... | collective-permute-start | bytes 12296 | tf_op jit(solution)/shard_map/ppermute | solution.py:443
  69.7 0.8 collective-permute-done.2.s3
  70.5 26.9 %scatter_points.1 = (f32[264,512]{1,0:T(8,128)S(1)}, f32[264,512]{1,0:T(8,128)S(1)}, f32[2,264,512]{2,1,0:T(8,128)S(1)}) custom-call(s32[64,128]{1,0:T(8,128)S(1)} %get-tuple-element.26.rows, s32[64,128]{1,0:T(8,128)S(1)} %get-tuple-element.27.lanes, f32[64,8,128]{2,1,0:T(8,128)S(1)} %broadcast_multiply_fusion.beta, f32[8,128]{1,0:T(8,128)S(1)} %gather_points.1.s0, ...), custom_call_target="tpu_custom_call" | custom-call | flops 104857600 | bytes 83886080 | tf_op jit(solution)/shard_map/scatter_points/pallas_call | solution.py:213
  97.4 1.6 %collective-permute-start.5 = (f32[264,512]{1,0:T(8,128)S(1)}, f32[264,512]{1,0:T(8,128)S(1)}, u32[]{:S(2)}, u32[]{:S(2)}) collective-permute-start(f32[264,512]{1,0:T(8,128)S(1)} %get-tuple-element.17.d3), channel_id=1, source_target_pairs={{0,1},{1,2},{2,3},{3,4},{4,5},{5,6},{6,7},{7,8},{8,9},{9,10},{10,1... | collective-permute-start | bytes 1622024 | tf_op jit(solution)/shard_map/ppermute | solution.py:447
  99.0 4.7 %collective-permute-start.6 = (f32[264,512]{1,0:T(8,128)S(1)}, f32[264,512]{1,0:T(8,128)S(1)}, u32[]{:S(2)}, u32[]{:S(2)}) collective-permute-start(f32[264,512]{1,0:T(8,128)S(1)} %get-tuple-element.18.d0), channel_id=1, source_target_pairs={{1,0},{2,1},{3,2},{4,3},{5,4},{6,5},{7,6},{8,7},{9,8},{10,9},{11,1... | collective-permute-start | bytes 1622024 | tf_op jit(solution)/shard_map/ppermute | solution.py:446
  103.8 8.8 %inner_planes.1 = (f32[8,128,512]{2,1,0:T(8,128)}, f32[128,512]{1,0:T(8,128)S(1)}, f32[128,512]{1,0:T(8,128)S(1)}) custom-call(f32[264,512]{1,0:T(8,128)S(1)} %get-tuple-element.18.d0, f32[264,512]{1,0:T(8,128)S(1)} %get-tuple-element.17.d3, f32[2,2,264,512]{3,2,1,0:T(8,128)S(1)} %get-tuple-element.19.keep, f32[2,2,264,512]{3,2,1,0:T(8,128)S(1)} %copy-done.4, ...), custom_call_target="tpu_custom_call" | custom-call | flops 104857600 | bytes 31457280 | tf_op jit(solution)/shard_map/inner_planes/pallas_call | solution.py:321
  112.5 3.5 %collective-permute-done.5.below = f32[264,512]{1,0:T(8,128)S(1)} collective-permute-done((f32[264,512]{1,0:T(8,128)S(1)}, f32[264,512]{1,0:T(8,128)S(1)}, u32[]{:S(2)}, u32[]{:S(2)}) %collective-permute-start.5) | collective-permute-done | bytes 540704 | tf_op jit(solution)/shard_map/ppermute | solution.py:447
  116.0 4.9 %outer_planes.1 = f32[8,128,512]{2,1,0:T(8,128)} custom-call(f32[264,512]{1,0:T(8,128)S(1)} %collective-permute-done.5.below, f32[264,512]{1,0:T(8,128)S(1)} %get-tuple-element.18.d0, f32[264,512]{1,0:T(8,128)S(1)} %get-tuple-element.17.d3, f32[264,512]{1,0:T(8,128)S(1)} %collective-permute-done.6.above, ...), custom_call_target="tpu_custom_call", output_to_operand_aliasing={{}: (4, {})} | custom-call | flops 104857600 | bytes 31457280 | tf_op jit(solution)/shard_map/outer_planes/pallas_call | solution.py:388
  (29 shorter events, 1.0 us)
Async XLA Ops:
  0.7 5.8 %copy-start = (f32[2,8,512,512]{3,2,1,0:T(8,128)S(1)}, f32[2,8,512,512]{3,2,1,0:T(8,128)}, u32[]{:S(2)}) copy-start(f32[2,8,512,512]{3,2,1,0:T(8,128)} %orb_ref.3) | copy-start | bytes 50331652
  6.5 1.6 %copy-start.2 = (f32[8,128,512]{2,1,0:T(8,128)S(1)}, f32[8,128,512]{2,1,0:T(8,128)}, u32[]{:S(2)}) copy-start(f32[8,128,512]{2,1,0:T(8,128)} %core_ref.3) | copy-start | bytes 6291460
  11.0 4.3 %copy-start.5 = (f32[2,2,264,512]{3,2,1,0:T(8,128)}, f32[2,2,264,512]{3,2,1,0:T(8,128)S(1)}, u32[]{:S(2)}) copy-start(f32[2,2,264,512]{3,2,1,0:T(8,128)S(1)} %get-tuple-element.15.keep) | copy-start | bytes 6488068
  11.0 4.3 %collective-permute-start.3 = (f32[2,2,264,512]{3,2,1,0:T(8,128)S(1)}, f32[2,2,264,512]{3,2,1,0:T(8,128)S(1)}, u32[]{:S(2)}, u32[]{:S(2)}) collective-permute-start(f32[2,2,264,512]{3,2,1,0:T(8,128)S(1)} %get-tuple-element.16), channel_id=1, source_target_pairs={{0,32},{32,0},{64,96},{96,64},{1,33},{33,1},{65,97},{97,65},{2,34}... | collective-permute-start | bytes 6488072 | tf_op jit(solution)/shard_map/ppermute | solution.py:417
  14.1 6.6 %collective-permute-start.7 = (f32[2,2,264,512]{3,2,1,0:T(8,128)S(1)}, f32[2,2,264,512]{3,2,1,0:T(8,128)S(1)}, u32[]{:S(2)}, u32[]{:S(2)}) collective-permute-start(f32[2,2,264,512]{3,2,1,0:T(8,128)S(1)} %get-tuple-element.20), channel_id=1, source_target_pairs={{0,32},{32,0},{64,96},{96,64},{1,33},{33,1},{65,97},{97,65},{2,34}... | collective-permute-start | bytes 6488072 | tf_op jit(solution)/shard_map/ppermute | solution.py:419
  15.4 6.5 %copy-start.7 = (f32[2,2,264,512]{3,2,1,0:T(8,128)}, f32[2,2,264,512]{3,2,1,0:T(8,128)S(1)}, u32[]{:S(2)}) copy-start(f32[2,2,264,512]{3,2,1,0:T(8,128)S(1)} %collective-permute-done.3.recv) | copy-start | bytes 6488068
  16.7 8.4 %copy-start.10 = (s32[64]{0:T(128)S(1)}, s32[64]{0:T(128)}, u32[]{:S(2)}) copy-start(s32[64]{0:T(128)} %param.11) | copy-start | bytes 772
  16.7 9.3 %copy-start.9 = (f32[64,8,128]{2,1,0:T(8,128)S(1)}, f32[64,8,128]{2,1,0:T(8,128)}, u32[]{:S(2)}) copy-start(f32[64,8,128]{2,1,0:T(8,128)} %param.9) | copy-start | bytes 786436
  16.7 53.8 %collective-permute-start.4 = (f32[2,264,512]{2,1,0:T(8,128)}, f32[2,264,512]{2,1,0:T(8,128)S(1)}, u32[]{:S(2)}, u32[]{:S(2)}) collective-permute-start(f32[2,264,512]{2,1,0:T(8,128)} %fusion.1), channel_id=1, source_target_pairs={{0,64},{64,0},{32,96},{96,32},{1,65},{65,1},{33,97},{97,33},{2,66}... | collective-permute-start | bytes 3244040 | tf_op jit(solution)/shard_map/ppermute | solution.py:420
  21.9 1.4 %copy-start.3 = (f32[2,2,264,512]{3,2,1,0:T(8,128)}, f32[2,2,264,512]{3,2,1,0:T(8,128)S(1)}, u32[]{:S(2)}) copy-start(f32[2,2,264,512]{3,2,1,0:T(8,128)S(1)} %collective-permute-done.7.recv) | copy-start | bytes 6488068
  23.3 80.5 %collective-permute-start.8 = (f32[2,264,512]{2,1,0:T(8,128)}, f32[2,264,512]{2,1,0:T(8,128)}, u32[]{:S(2)}, u32[]{:S(2)}) collective-permute-start(f32[2,264,512]{2,1,0:T(8,128)} %fusion), channel_id=1, source_target_pairs={{0,64},{64,0},{32,96},{96,32},{1,65},{65,1},{33,97},{97,33},{2,66}... | collective-permute-start | bytes 3244040 | tf_op jit(solution)/shard_map/ppermute | solution.py:421
  26.0 5.8 %copy-start.1 = (f32[2,8,512,512]{3,2,1,0:T(8,128)S(1)}, f32[2,8,512,512]{3,2,1,0:T(8,128)}, u32[]{:S(2)}) copy-start(f32[2,8,512,512]{3,2,1,0:T(8,128)} %orb_ref.3) | copy-start | bytes 50331652
  31.8 38.7 %copy-start.6 = (f32[2,2,264,512]{3,2,1,0:T(8,128)S(1)}, f32[2,2,264,512]{3,2,1,0:T(8,128)}, u32[]{:S(2)}) copy-start(f32[2,2,264,512]{3,2,1,0:T(8,128)} %copy-done.5) | copy-start | bytes 6488068
  31.8 38.7 %copy-start.8 = (f32[2,2,264,512]{3,2,1,0:T(8,128)S(1)}, f32[2,2,264,512]{3,2,1,0:T(8,128)}, u32[]{:S(2)}) copy-start(f32[2,2,264,512]{3,2,1,0:T(8,128)} %copy-done.7) | copy-start | bytes 6488068
  64.4 4.8 %collective-permute-start = (f32[8,128]{1,0:T(8,128)S(1)}, f32[8,128]{1,0:T(8,128)S(1)}, u32[]{:S(2)}, u32[]{:S(2)}) collective-permute-start(f32[8,128]{1,0:T(8,128)S(1)} %gather_points.1.s0), channel_id=1, source_target_pairs={{0,32},{32,64},{64,96},{96,0},{1,33},{33,65},{65,97},{97,1},{2,34}... | collective-permute-start | bytes 12296 | tf_op jit(solution)/shard_map/ppermute | solution.py:443
  64.5 5.1 %collective-permute-start.1 = (f32[8,128]{1,0:T(8,128)S(1)}, f32[8,128]{1,0:T(8,128)S(1)}, u32[]{:S(2)}, u32[]{:S(2)}) collective-permute-start(f32[8,128]{1,0:T(8,128)S(1)} %gather_points.1.s0), channel_id=1, source_target_pairs={{0,64},{32,96},{64,0},{96,32},{1,65},{33,97},{65,1},{97,33},{2,66}... | collective-permute-start | bytes 12296 | tf_op jit(solution)/shard_map/ppermute | solution.py:443
  66.3 4.2 %collective-permute-start.2 = (f32[8,128]{1,0:T(8,128)S(1)}, f32[8,128]{1,0:T(8,128)S(1)}, u32[]{:S(2)}, u32[]{:S(2)}) collective-permute-start(f32[8,128]{1,0:T(8,128)S(1)} %gather_points.1.s0), channel_id=1, source_target_pairs={{0,96},{32,0},{64,32},{96,64},{1,97},{33,1},{65,33},{97,65},{2,98}... | collective-permute-start | bytes 12296 | tf_op jit(solution)/shard_map/ppermute | solution.py:443
  70.5 33.3 %copy-start.4 = (f32[2,2,264,512]{3,2,1,0:T(8,128)S(1)}, f32[2,2,264,512]{3,2,1,0:T(8,128)}, u32[]{:S(2)}) copy-start(f32[2,2,264,512]{3,2,1,0:T(8,128)} %copy-done.3) | copy-start | bytes 6488068
  97.4 18.6 %collective-permute-start.5 = (f32[264,512]{1,0:T(8,128)S(1)}, f32[264,512]{1,0:T(8,128)S(1)}, u32[]{:S(2)}, u32[]{:S(2)}) collective-permute-start(f32[264,512]{1,0:T(8,128)S(1)} %get-tuple-element.17.d3), channel_id=1, source_target_pairs={{0,1},{1,2},{2,3},{3,4},{4,5},{5,6},{6,7},{7,8},{8,9},{9,10},{10,1... | collective-permute-start | bytes 1622024 | tf_op jit(solution)/shard_map/ppermute | solution.py:447
  99.0 17.0 %collective-permute-start.6 = (f32[264,512]{1,0:T(8,128)S(1)}, f32[264,512]{1,0:T(8,128)S(1)}, u32[]{:S(2)}, u32[]{:S(2)}) collective-permute-start(f32[264,512]{1,0:T(8,128)S(1)} %get-tuple-element.18.d0), channel_id=1, source_target_pairs={{1,0},{2,1},{3,2},{4,3},{5,4},{6,5},{7,6},{8,7},{9,8},{10,9},{11,1... | collective-permute-start | bytes 1622024 | tf_op jit(solution)/shard_map/ppermute | solution.py:446

commit v2 on v1

v2 whole, which is shorter than its diff:
```python
import functools
import math

import jax
import jax.numpy as jnp
from jax import lax
from jax.experimental import pallas as pl
from jax.experimental.pallas import tpu as pltpu
from jax.sharding import PartitionSpec as P

f32 = jnp.float32
bf16 = jnp.bfloat16
i32 = jnp.int32

coef_a = 0.75 * (3.0 / math.pi) ** (1.0 / 3.0)
kappa_val = 0.804
mu_val = 0.2195149727645171
s_scale = 4.0 * (3.0 * math.pi**2) ** (2.0 / 3.0)
LOG2E = math.log2(math.e)

MIB = 2**20
GROUP = 264
LOW = 256
HIGH = 260
ACC_ROWS = 16 * GROUP
N_ACC = 8
NT = (((1,), (1,)), ((), ()))
VM = pl.BlockSpec(memory_space=pltpu.VMEM)
SM = pl.BlockSpec(memory_space=pltpu.SMEM)
ANY = pl.BlockSpec(memory_space=pl.ANY)
HBM = pl.BlockSpec(memory_space=pltpu.HBM)


def params(mib):
    return pltpu.CompilerParams(vmem_limit_bytes=mib * MIB)


MESH = pl.DeviceIdType.MESH
STEP = 8
ORDER = (0, 3, 1, 2)
TILES = GROUP // 8 * 4


def front_kernel(
    weights, rows, lanes, beta, core, orb,
    w_ref, outer_ref, near_ref, far_ref,
    buf, picked, keep, send, recv, come, w_mine, w_core, w_come,
    load_sem, swap_out, swap_in, far_out, far_in, w_out, w_in,
):
    band = lax.axis_index("band")
    dom = lax.axis_index("dom")
    parity = lax.rem(band, 2)
    z_hi = band // 2
    mate = (band + 1 - 2 * parity, dom)
    opposite = (lax.rem(band + 2, 4), dom)

    def loads(gi):
        made = []
        for i in range(2):
            x = 2 * ORDER[gi] + i
            for o in range(2):
                made.append(
                    pltpu.make_async_copy(
                        orb.at[o, x], buf.at[pl.ds(256 * x, 256), o], load_sem.at[4 * gi + 2 * i + o]
                    )
                )
        return made

    for gi in range(2):
        for copy in loads(gi):
            copy.start()
    barrier = pltpu.get_barrier_semaphore()
    for partner in (mate, opposite):
        pl.semaphore_signal(barrier, inc=1, device_id=partner, device_id_type=MESH)
    w0 = weights[0]
    w1 = weights[1]

    def squares(tile, count):
        a = buf[pl.ds(tile, count), 0]
        b = buf[pl.ds(tile, count), 1]
        return w0 * a * a + w1 * b * b

    def fill(ref, gi, near, mine):
        q = 2 * (z_hi if near else 1 - z_hi) + (parity if mine else 1 - parity)
        for i in range(2):
            x = 2 * ORDER[gi] + i

            def body(j, _):
                value = squares(x * 256 + q * 64 + 16 * j, 16)
                if near and mine:
                    value = value + core[x, pl.ds(16 * j, 16)]
                ref[near, gi, pl.ds(64 * i + 16 * j, 16)] = value
                return 0

            lax.fori_loop(0, 4, body, 0)
            q_low = lax.rem(q + 3, 4)
            own = jnp.where(q_low == band, 1.0, 0.0)
            value = squares(x * 256 + q_low * 64 + 60, 4) + own * core[x, 60:64]
            ref[near, gi, 128:132, 2 * i : 2 * i + 2, :] = value[:, 6:8, :]
            q_high = lax.rem(q + 1, 4)
            own = jnp.where(q_high == band, 1.0, 0.0)
            value = squares(x * 256 + q_high * 64, 4) + own * core[x, 0:4]
            ref[near, gi, 128:132, 4 + 2 * i : 6 + 2 * i, :] = value[:, 0:2, :]

    def swap(near, gi):
        return pltpu.make_async_remote_copy(
            src_ref=send.at[near, gi],
            dst_ref=recv.at[near, gi],
            send_sem=swap_out.at[4 * near + gi],
            recv_sem=swap_in.at[4 * near + gi],
            device_id=mate,
            device_id_type=MESH,
        )

    def across(gi):
        return pltpu.make_async_remote_copy(
            src_ref=keep.at[0, gi],
            dst_ref=come.at[gi],
            send_sem=far_out.at[gi],
            recv_sem=far_in.at[gi],
            device_id=opposite,
            device_id_type=MESH,
        )

    def summed(near, gi, put):
        def body(j, _):
            here = pl.ds(12 * j, 12)
            put(here, keep[near, gi, here] + recv[near, gi, here])
            return 0

        lax.fori_loop(0, TILES // 12, body, 0)

    for gi in range(4):
        for copy in loads(gi):
            copy.wait()
        if gi < 2:
            for copy in loads(gi + 2):
                copy.start()
        fill(send, gi, 0, False)
        if gi == 0:
            pl.semaphore_wait(barrier, 2)
        swap(0, gi).start()
        fill(keep, gi, 0, True)
        fill(send, gi, 1, False)
        swap(1, gi).start()
        fill(keep, gi, 1, True)
        swap(0, gi).wait()

        def put_far(here, value):
            keep[0, gi, here] = value

        def put_out(here, value):
            far_ref[gi - 2, here] = value

        summed(0, gi, put_far if gi < 2 else put_out)
        if gi < 2:
            across(gi).start()

    flat = buf.reshape(32768, 128)
    sub = lax.broadcasted_iota(i32, (128, 128), 0)
    two = lax.broadcasted_iota(i32, (256, 128), 0) - 2 * lax.broadcasted_iota(i32, (256, 128), 1)
    even = two == 0
    odd = two == 1
    lane_ids = lax.broadcasted_iota(i32, (8, 128), 1)

    def step(i, total):
        for j in range(STEP):
            for k in range(128):
                r = rows[STEP * i + j, k]
                picked[pl.ds(256 * j + 2 * k, 2), :] = flat[pl.ds(r, 2, stride=8), :]
        for j in range(STEP):
            b = STEP * i + j
            hot = jnp.where(lanes[pl.ds(b, 1), :] == sub, 1.0, 0.0).astype(bf16)
            g = picked[256 * j : 256 * j + 256]
            g1 = g.astype(bf16)
            g2 = (g - g1.astype(f32)).astype(bf16)
            t = jnp.dot(g1, hot, preferred_element_type=f32) + jnp.dot(g2, hot, preferred_element_type=f32)
            be = beta[b]
            p0 = jnp.sum(jnp.where(even, t, 0.0), axis=0, keepdims=True)
            p1 = jnp.sum(jnp.where(odd, t, 0.0), axis=0, keepdims=True)
            c0 = jnp.sum(be * p0, axis=1, keepdims=True)
            c1 = jnp.sum(be * p1, axis=1, keepdims=True)
            total = jnp.where(lane_ids == b, w0 * c0 * c0 + w1 * c1 * c1, total)
        return total

    w_mine[...] = lax.fori_loop(0, 64 // STEP, step, jnp.zeros((8, 128), f32))

    def send_w(src, dst, at, target):
        return pltpu.make_async_remote_copy(
            src_ref=src,
            dst_ref=dst,
            send_sem=w_out.at[at],
            recv_sem=w_in.at[at],
            device_id=target,
            device_id_type=MESH,
        )

    first = send_w(w_mine, w_come.at[0], 0, mate)
    first.start()
    for gi in range(4):
        swap(1, gi).wait()

        def put_near(here, value):
            near_ref[gi - 2, here] = value

        def put_keep(here, value):
            keep[1, gi, here] = value

        summed(1, gi, put_keep if gi < 2 else put_near)
    first.wait()
    w_core[...] = w_mine[...] + w_come[0]
    second = send_w(w_core, w_come.at[1], 1, opposite)
    second.start()
    for gi in range(2):
        across(gi).wait()

        def body(j, _):
            here = pl.ds(12 * j, 12)
            outer_ref[gi, here] = keep[1, gi, here] + come[gi, here]
            return 0

        lax.fori_loop(0, TILES // 12, body, 0)
    second.wait()
    w_ref[...] = w_core[...] + w_come[1]


def front(weights, rows, lanes, beta, core, orbitals):
    tiles = orbitals.reshape(2, 8, 64, 8, 4, 128).transpose(0, 1, 2, 4, 3, 5).reshape(2, 8, 256, 8, 128)
    core = core.reshape(8, 16, 8, 4, 128).transpose(0, 1, 3, 2, 4).reshape(8, 64, 8, 128)
    pair = jax.ShapeDtypeStruct((2, TILES, 8, 128), f32)
    both = pltpu.VMEM((2, 4, TILES, 8, 128), f32)
    strengths = pltpu.VMEM((8, 128), f32)
    dma = pltpu.SemaphoreType.DMA
    w, outer_sum, near, far = pl.pallas_call(
        front_kernel,
        in_specs=[SM, SM, VM, VM, VM, HBM],
        out_specs=[VM] * 4,
        out_shape=[jax.ShapeDtypeStruct((8, 128), f32), pair, pair, pair],
        scratch_shapes=[
            pltpu.VMEM((2048, 2, 8, 128), f32),
            pltpu.VMEM((256 * STEP, 128), f32),
            both,
            both,
            both,
            pltpu.VMEM((2, TILES, 8, 128), f32),
            strengths,
            strengths,
            pltpu.VMEM((2, 8, 128), f32),
            dma((16,)),
            dma((8,)),
            dma((8,)),
            dma((2,)),
            dma((2,)),
            dma((2,)),
            dma((2,)),
        ],
        compiler_params=pltpu.CompilerParams(
            vmem_limit_bytes=60 * MIB, collective_id=0, has_side_effects=True
        ),
        cost_estimate=pl.CostEstimate(flops=100 * MIB, bytes_accessed=40 * MIB, transcendentals=0),
        name="front",
    )(weights, rows, lanes, beta, core, tiles)
    plain = lambda t: t.reshape(2, 33, 4, 8, 128).transpose(0, 1, 3, 2, 4).reshape(2, GROUP, 512)
    return w, plain(outer_sum), plain(near), plain(far)


def scatter_kernel(
    rows, lanes, beta, strength_ref, sums, d0_ref, d3_ref, aug_ref, spread, *accs
):
    for acc in accs:
        acc[...] = jnp.zeros_like(acc)
    strengths = strength_ref[...]
    sub = lax.broadcasted_iota(i32, (128, 128), 0)
    eye = sub == lax.broadcasted_iota(i32, (128, 128), 1)
    lane_ids = lax.broadcasted_iota(i32, (8, 128), 1)

    def spread_step(i, _):
        for j in range(STEP):
            b = STEP * i + j
            be = beta[b]
            w = jnp.sum(jnp.where(lane_ids == b, strengths, 0.0), axis=1, keepdims=True)
            at = jnp.sum(w * be * be, axis=0, keepdims=True)
            a1 = at.astype(bf16).astype(f32)
            hot = jnp.where(lanes[pl.ds(b, 1), :] == sub, 1.0, 0.0).astype(bf16)
            d1 = jnp.where(eye, a1, 0.0).astype(bf16)
            d2 = jnp.where(eye, at - a1, 0.0).astype(bf16)
            spread[pl.ds(pl.multiple_of(b * 128, 128), 128), :] = lax.dot_general(
                d1, hot, NT, preferred_element_type=f32
            ) + lax.dot_general(d2, hot, NT, preferred_element_type=f32)
        return 0

    lax.fori_loop(0, 64 // STEP, spread_step, 0)

    def add_step(b, _):
        first = pl.multiple_of(b * 128, 128)
        for k in range(0, 128, N_ACC):
            at_rows = [rows[b, k + j] for j in range(N_ACC)]
            old = [accs[j][pl.ds(at_rows[j], 1), :] for j in range(N_ACC)]
            for j in range(N_ACC):
                accs[j][pl.ds(at_rows[j], 1), :] = old[j] + spread[pl.ds(first + k + j, 1), :]
        return 0

    lax.fori_loop(0, 64, add_step, 0)

    def summed(g, c):
        piece = pl.ds((g * 4 + c) * GROUP, GROUP)
        total = accs[0][piece, :]
        for acc in accs[1:]:
            total = total + acc[piece, :]
        return total

    for at, g, ref in ((0, 0, d0_ref), (1, 3, d3_ref)):
        for c in range(4):
            cols = slice(128 * c, 128 * c + 128)
            ref[:, cols] = sums[at, :, cols] + summed(g, c)
    for at, g in ((0, 1), (1, 2)):
        for c in range(4):
            aug_ref[at, :, 128 * c : 128 * c + 128] = summed(g, c)


def scatter(rows, lanes, beta, strengths, sums):
    group = jax.ShapeDtypeStruct((GROUP, 512), f32)
    whole2 = lambda *shape: pl.BlockSpec(shape, lambda s: (0,) * len(shape))
    return pl.pallas_call(
        scatter_kernel,
        grid=(1,),
        in_specs=[
            SM,
            whole2(64, 128),
            whole2(64, 8, 128),
            whole2(8, 128),
            whole2(2, GROUP, 512),
        ],
        out_specs=[whole2(GROUP, 512), whole2(GROUP, 512), whole2(2, GROUP, 512)],
        out_shape=[group, group, jax.ShapeDtypeStruct((2, GROUP, 512), f32)],
        scratch_shapes=[pltpu.VMEM((8192, 128), f32)] + [pltpu.VMEM((ACC_ROWS + 8, 128), f32)] * N_ACC,
        compiler_params=params(60),
        cost_estimate=pl.CostEstimate(flops=100 * MIB, bytes_accessed=80 * MIB, transcendentals=0),
        name="scatter_points",
    )(rows, lanes, beta, strengths, sums)


def place_group(dens, plane, group, lead=None):
    for i in range(2):
        dens[plane + i, 16:144, :] = group[pl.ds(128 * i, 128), :]
        dens[plane + i, 14:16, :] = group[pl.ds(LOW + 2 * i, 2), :]
        dens[plane + i, 144:146, :] = group[pl.ds(HIGH + 2 * i, 2), :]


def local_parts(dens, x, row, count):
    mid = dens[x, pl.ds(row, count), :]
    gy = (dens[x, pl.ds(row + 1, count), :] - dens[x, pl.ds(row - 1, count), :]) * 0.5
    gx = (dens[x + 1, pl.ds(row, count), :] - dens[x - 1, pl.ds(row, count), :]) * 0.5
    gz = (pltpu.roll(mid, 511, 1) - pltpu.roll(mid, 1, 1)) * 0.5
    sigma = gy * gy + gx * gx + gz * gz
    logs = jnp.log(mid)
    cube = jnp.exp2(logs * (LOG2E / 3.0))
    inv_four = jnp.exp2(logs * (-4.0 * LOG2E / 3.0))
    reduced = sigma * (inv_four * inv_four) * (1.0 / s_scale)
    under = 1.0 + (mu_val / kappa_val) * reduced
    inv = pl.reciprocal(under, approx=True)
    inv = inv * (2.0 - under * inv)
    slope = mu_val * inv * inv
    factor = (1.0 + kappa_val) - kappa_val * inv
    e_n = (-4.0 / 3.0 * coef_a) * cube * (factor - 2.0 * reduced * slope)
    twice = (-2.0 * coef_a / s_scale) * inv_four * slope
    return e_n, twice * gy, twice * gx, twice * gz


STRIP = 16


def full_plane(dens, x, flux_y, put):
    for row in (8, 144):
        flux_y[pl.ds(row, 8), :] = local_parts(dens, x, row, 8)[1]
    for row in range(16, 144, STRIP):
        e_n, fy, fx, fz = local_parts(dens, x, row, STRIP)
        flux_y[pl.ds(row, STRIP), :] = fy
        put(row - 16, e_n - (pltpu.roll(fz, 511, 1) - pltpu.roll(fz, 1, 1)) * 0.5, fx)


def minus_y(flux_y, row):
    up = flux_y[pl.ds(row + 17, STRIP), :]
    down = flux_y[pl.ds(row + 15, STRIP), :]
    return (up - down) * 0.5


def inner_kernel(d0, d3, near, far, aug, pot_ref, low_ref, high_ref, dens, flux_x, flux_y):
    place_group(dens, 0, d0)
    place_group(dens, 6, d3)
    for g in range(2):
        total = near[g] + far[g] + aug[g]
        for i in range(2):
            dens[2 + 2 * g + i, 16:144, :] = total[128 * i : 128 * i + 128]
            dens[2 + 2 * g + i, 14:16, :] = total[LOW + 2 * i : LOW + 2 * i + 2]
            dens[2 + 2 * g + i, 144:146, :] = total[HIGH + 2 * i : HIGH + 2 * i + 2]

    def plane(x, _):
        def put(row, value, fx):
            pot_ref[x, pl.ds(row, STRIP), :] = value
            flux_x[x, pl.ds(row, STRIP), :] = fx

        full_plane(dens, x, flux_y, put)
        for row in range(0, 128, STRIP):
            here = pl.ds(row, STRIP)
            pot_ref[x, here, :] = pot_ref[x, here, :] - minus_y(flux_y, row)
        return 0

    lax.fori_loop(1, 7, plane, 0)

    def across(x, _):
        for row in range(0, 128, STRIP):
            here = pl.ds(row, STRIP)
            pot_ref[x, here, :] = (
                pot_ref[x, here, :] - (flux_x[x + 1, here, :] - flux_x[x - 1, here, :]) * 0.5
            )
        return 0

    lax.fori_loop(2, 6, across, 0)
    pot_ref[1] = pot_ref[1] - flux_x[2] * 0.5
    pot_ref[6] = pot_ref[6] + flux_x[5] * 0.5
    pot_ref[0] = jnp.zeros((128, 512), f32)
    pot_ref[7] = jnp.zeros((128, 512), f32)
    low_ref[...] = flux_x[1]
    high_ref[...] = flux_x[6]


def inner(d0, d3, near, far, aug):
    whole2 = lambda *shape: pl.BlockSpec(shape, lambda s: (0,) * len(shape))
    plane = jax.ShapeDtypeStruct((128, 512), f32)
    return pl.pallas_call(
        inner_kernel,
        grid=(1,),
        in_specs=[whole2(GROUP, 512)] * 2 + [whole2(2, GROUP, 512)] * 3,
        out_specs=[whole2(8, 128, 512), whole2(128, 512), whole2(128, 512)],
        out_shape=[jax.ShapeDtypeStruct((8, 128, 512), f32), plane, plane],
        scratch_shapes=[
            pltpu.VMEM((8, 160, 512), f32),
            pltpu.VMEM((8, 128, 512), f32),
            pltpu.VMEM((160, 512), f32),
        ],
        compiler_params=params(60),
        cost_estimate=pl.CostEstimate(flops=100 * MIB, bytes_accessed=30 * MIB, transcendentals=0),
        name="inner_planes",
    )(d0, d3, near, far, aug)


def outer_kernel(below, d0, d3, above, old, low, high, pot_ref, dens, flux_x, flux_y):
    place_group(dens, 0, below)
    place_group(dens, 2, d0)
    place_group(dens, 4, d3)
    place_group(dens, 6, above)
    for row in range(0, 128, STRIP):
        flux_x[0, pl.ds(row, STRIP), :] = local_parts(dens, 1, row + 16, STRIP)[2]
        flux_x[1, pl.ds(row, STRIP), :] = local_parts(dens, 6, row + 16, STRIP)[2]

    for end, x, edge, inside in ((0, 2, 0, 1), (1, 5, 3, 2)):

        def put(row, value, fx):
            here = pl.ds(row, STRIP)
            pot_ref[edge, here, :] = value
            if end == 0:
                pot_ref[inside, here, :] = old[1, here, :] + 0.5 * fx
            else:
                pot_ref[inside, here, :] = old[2, here, :] - 0.5 * fx

        full_plane(dens, x, flux_y, put)
        for row in range(0, 128, STRIP):
            here = pl.ds(row, STRIP)
            if end == 0:
                across = (low[here, :] - flux_x[0, here, :]) * 0.5
            else:
                across = (flux_x[1, here, :] - high[here, :]) * 0.5
            pot_ref[edge, here, :] = pot_ref[edge, here, :] - minus_y(flux_y, row) - across


def outer_body(below, d0, d3, above, old_ref, low, high, pot_ref, dens, flux_x, flux_y, old, new, sem):
    ins = [
        pltpu.make_async_copy(old_ref.at[pl.ds(0, 2)], old.at[pl.ds(0, 2)], sem.at[0]),
        pltpu.make_async_copy(old_ref.at[pl.ds(6, 2)], old.at[pl.ds(2, 2)], sem.at[1]),
    ]
    for copy in ins:
        copy.start()
    for copy in ins:
        copy.wait()
    outer_kernel(below, d0, d3, above, old, low, high, new, dens, flux_x, flux_y)
    outs = [
        pltpu.make_async_copy(new.at[pl.ds(0, 2)], pot_ref.at[pl.ds(0, 2)], sem.at[2]),
        pltpu.make_async_copy(new.at[pl.ds(2, 2)], pot_ref.at[pl.ds(6, 2)], sem.at[3]),
    ]
    for copy in outs:
        copy.start()
    for copy in outs:
        copy.wait()


def outer(below, d0, d3, above, old, low, high):
    return pl.pallas_call(
        outer_body,
        in_specs=[VM, VM, VM, VM, ANY, VM, VM],
        out_specs=ANY,
        out_shape=jax.ShapeDtypeStruct((8, 128, 512), f32),
        input_output_aliases={4: 0},
        scratch_shapes=[
            pltpu.VMEM((8, 160, 512), f32),
            pltpu.VMEM((2, 128, 512), f32),
            pltpu.VMEM((160, 512), f32),
            pltpu.VMEM((4, 128, 512), f32),
            pltpu.VMEM((4, 128, 512), f32),
            pltpu.SemaphoreType.DMA((4,)),
        ],
        compiler_params=params(60),
        cost_estimate=pl.CostEstimate(flops=100 * MIB, bytes_accessed=30 * MIB, transcendentals=0),
        name="outer_planes",
    )(below, d0, d3, above, old, low, high)


def shards(orbitals, occupation, core_density, proj_values, block_index, live_points):
    band = lax.axis_index("band")
    weights = occupation.astype(f32) * 0.001
    far_pairs = [(0, 2), (2, 0), (1, 3), (3, 1)]

    point_ids = lax.broadcasted_iota(i32, block_index.shape, 1)
    beta = proj_values * (point_ids < live_points[:, None]).astype(f32)[:, None, :]
    x = block_index >> 18
    y = (block_index >> 9) & 511
    c = (block_index >> 7) & 3
    lanes = block_index & 127
    from_rows = ((x * 64 + (y >> 3)) * 4 + c) * 16 + (y & 7)
    own = (y - 128 * band) & 511
    pair = (x & 1) * 2
    inside = jnp.where(
        own < 128,
        (x & 1) * 128 + own,
        jnp.where(own >= 510, LOW + pair + own - 510, HIGH + pair + own - 128),
    )
    into_rows = jnp.where(
        (own < 130) | (own >= 510), ((x >> 1) * 4 + c) * GROUP + inside, ACC_ROWS
    )

    strengths, outer_sum, near, far = front(
        weights, from_rows, lanes, beta, core_density, orbitals
    )
    far = lax.ppermute(far, "band", far_pairs)
    d0, d3, aug = scatter(into_rows, lanes, beta, strengths, outer_sum)
    above = lax.ppermute(d0, "dom", [((i + 1) % 32, i) for i in range(32)])
    below = lax.ppermute(d3, "dom", [(i, (i + 1) % 32) for i in range(32)])
    part, low, high = inner(d0, d3, near, far, aug)
    return outer(below, d0, d3, above, part, low, high)


def solution(mesh):
    placed = (
        P("band", "dom", None, None),
        P("band"),
        P("dom", "band", None),
        P("dom", None, None),
        P("dom", None),
        P("dom"),
    )
    return jax.shard_map(
        shards, mesh=mesh, in_specs=placed, out_specs=P("dom", "band", None), check_vma=False
    )
```

time: 123 us -> 99.3 us (0.81); the launches traced: 121 us -> 99 us
  local copies, waits for them, and re-layouts: 14.6 us -> 1.95 us
  Pallas kernels: 79.1 us -> 68.8 us
  waiting for transfers between devices: 5.54 us -> 15.6 us
  starting transfers between devices: 17.5 us -> 7.56 us
    ppermute x7 -> x1, waiting for transfers between devices: 2.07 us -> 15.6 us  [shards(): far = lax.ppermute(far, 'band', far_pairs)]
    unnamed x22 -> x6, local copies, waits for them, and re-layouts: 14.6 us -> 1.95 us
    pallas_call x1, Pallas kernels: 26.9 us -> 15.8 us  [scatter(): pl.pallas_call(scatter_kernel, grid=(1,), in_specs=[SM, whole2(64, 128),...]
    ppermute x7 -> x1, starting transfers between devices: 11.2 us -> 1.32 us  [shards(): far = lax.ppermute(far, 'band', far_pairs)]
    ppermute x1, waiting for transfers between devices: 3.46 us -> 0.01 us  [shards(): below = lax.ppermute(d3, 'dom', [(i, (i + 1) % 32) for i in range(32)])]
    pallas_call x3 -> x1, Pallas kernels: 38.5 us -> 36.2 us  [front(): pl.pallas_call(front_kernel, in_specs=[SM, SM, VM, VM, VM, HBM], out_spec...]
    pallas_call x1, Pallas kernels: 4.93 us -> 6.88 us  [outer(): pl.pallas_call(outer_body, in_specs=[VM, VM, VM, VM, ANY, VM, VM], out_sp...]
    add x3 -> x1, other arithmetic: 3.34 us -> 1.43 us  [shards(): from_rows = ((x * 64 + (y >> 3)) * 4 + c) * 16 + (y & 7)]
  transfers between devices with their start and end apart: 9 -> 3, of which waited for: 4 -> 1; matrix products, arithmetic and copies ran while one was open for 3% -> 0% of each run, Pallas kernels for 59% -> 26%
where the time goes in v2:
time: 99.3 us; the launch traced here: 99 us
  Pallas kernels  68.8 us (69%)
  waiting for transfers between devices  15.6 us (16%)
  starting transfers between devices  7.56 us (8%)
  other arithmetic  5 us (5%)
  local copies, waits for them, and re-layouts  1.95 us (2%)
    pallas_call x1, Pallas kernels, front(): pl.pallas_call(front_kernel, in_specs=[SM, SM, VM, VM, VM, HBM], out_spec...  36.2 us
    pallas_call x1, Pallas kernels, scatter(): pl.pallas_call(scatter_kernel, grid=(1,), in_specs=[SM, whole2(64, 128),...  15.8 us
    ppermute x1, waiting for transfers between devices, shards(): far = lax.ppermute(far, 'band', far_pairs)  15.6 us
    pallas_call x1, Pallas kernels, inner(): pl.pallas_call(inner_kernel, grid=(1,), in_specs=[whole2(GROUP, 512)] * 2...  9.97 us
    pallas_call x1, Pallas kernels, outer(): pl.pallas_call(outer_body, in_specs=[VM, VM, VM, VM, ANY, VM, VM], out_sp...  6.88 us
    ppermute x1, starting transfers between devices, shards(): above = lax.ppermute(d0, 'dom', [((i + 1) % 32, i) for i in range(32)])  4.75 us
  transfers between devices with their start and end apart: 3, of which 1 were waited for; matrix products, arithmetic and copies ran while one was open for 0% of the time, Pallas kernels for 26%

profile of v2, /device:TPU:0, one launch (start us, length us, event | category | flops | bytes accessed | tf_op | source)
XLA Modules:
  0.0 99.0 jit_solution(9421590404057786654)
XLA Ops:
  0.0 0.7 fusion
  0.7 1.2 %convert_multiply_fusion.weights = f32[2]{0:T(128)} fusion(s32[2]{0:T(128)} %param.7), kind=kLoop, calls=%fused_computation.9 | loop fusion | flops 4 | bytes 16 | tf_op jit(solution)/shard_map/mul | solution.py:520
  1.9 1.4 %and_add_fusion = (s32[64,128]{1,0:T(8,128)}, s32[64,128]{1,0:T(8,128)}, s32[64,128]{1,0:T(8,128)}) fusion(s32[64,128]{1,0:T(8,128)} %param.10, s32[]{:T(128)S(6)} %mul.47), kind=kLoop, calls=%fused_computation.1 | loop fusion | flops 311296 | bytes 131076 | tf_op jit(solution)/shard_map/add | solution.py:529
  3.3 1.7 %broadcast_multiply_fusion.beta = f32[64,8,128]{2,1,0:T(8,128)} fusion(f32[64,8,128]{2,1,0:T(8,128)} %param.9, f32[64,128]{1,0:T(8,128)S(1)} %fusion), kind=kLoop, calls=%fused_computation | loop fusion | flops 65536 | bytes 557056 | tf_op jit(solution)/shard_map/mul | solution.py:524
  5.0 36.2 %front.1 = (f32[8,128]{1,0:T(8,128)}, f32[2,132,8,128]{3,2,1,0:T(8,128)}, f32[2,132,8,128]{3,2,1,0:T(8,128)}, f32[2,132,8,128]{3,2,1,0:T(8,128)}) custom-call(f32[2]{0:T(128)} %convert_multiply_fusion.weights, s32[64,128]{1,0:T(8,128)} %get-tuple-element.25.rows, s32[64,128]{1,0:T(8,128)} %get-tuple-element.27.lanes, ...), custom_call_target="tpu_custom_call" | custom-call | flops 104857600 | bytes 41943040 | tf_op jit(solution)/shard_map/front/pallas_call | solution.py:234
  41.2 1.3 %collective-permute-start.2 = (f32[2,264,512]{2,1,0:T(8,128)}, f32[2,264,512]{2,1,0:T(8,128)S(1)}, u32[]{:S(2)}, u32[]{:S(2)}) collective-permute-start(f32[2,264,512]{2,1,0:T(8,128)} %bitcast.29), channel_id=1, source_target_pairs={{0,64},{64,0},{32,96},{96,32},{1,65},{65,1},{33,97},{97,33},{2,66}... | collective-permute-start | bytes 3244040 | tf_op jit(solution)/shard_map/ppermute | solution.py:544
  42.6 15.8 %scatter_points.1 = (f32[264,512]{1,0:T(8,128)}, f32[264,512]{1,0:T(8,128)}, f32[2,264,512]{2,1,0:T(8,128)}) custom-call(s32[64,128]{1,0:T(8,128)} %get-tuple-element.26.rows, s32[64,128]{1,0:T(8,128)} %get-tuple-element.27.lanes, f32[64,8,128]{2,1,0:T(8,128)} %broadcast_multiply_fusion.beta, f32[8,128]{1,0:T(8,128)} %get-tuple-element.15.strength_ref, ...), custom_call_target="tpu_custom_call" | custom-call | flops 104857600 | bytes 83886080 | tf_op jit(solution)/shard_map/scatter_points/pallas_call | solution.py:324
  58.3 1.5 %collective-permute-start = (f32[264,512]{1,0:T(8,128)}, f32[264,512]{1,0:T(8,128)S(1)}, u32[]{:S(2)}, u32[]{:S(2)}) collective-permute-start(f32[264,512]{1,0:T(8,128)} %get-tuple-element.17.d3), channel_id=1, source_target_pairs={{0,1},{1,2},{2,3},{3,4},{4,5},{5,6},{6,7},{7,8},{8,9},{9,10},{10,1... | collective-permute-start | bytes 1622024 | tf_op jit(solution)/shard_map/ppermute | solution.py:547
  59.8 4.7 %collective-permute-start.1 = (f32[264,512]{1,0:T(8,128)}, f32[264,512]{1,0:T(8,128)S(1)}, u32[]{:S(2)}, u32[]{:S(2)}) collective-permute-start(f32[264,512]{1,0:T(8,128)} %get-tuple-element.18.d0), channel_id=1, source_target_pairs={{1,0},{2,1},{3,2},{4,3},{5,4},{6,5},{7,6},{8,7},{9,8},{10,9},{11,1... | collective-permute-start | bytes 1622024 | tf_op jit(solution)/shard_map/ppermute | solution.py:546
  64.6 15.6 %collective-permute-done.2.far = f32[2,264,512]{2,1,0:T(8,128)S(1)} collective-permute-done((f32[2,264,512]{2,1,0:T(8,128)}, f32[2,264,512]{2,1,0:T(8,128)S(1)}, u32[]{:S(2)}, u32[]{:S(2)}) %collective-permute-start.2) | collective-permute-done | bytes 1081376 | tf_op jit(solution)/shard_map/ppermute | solution.py:544
  80.1 0.0 copy-start
  80.1 1.0 copy-done
  81.1 10.0 %inner_planes.1 = (f32[8,128,512]{2,1,0:T(8,128)}, f32[128,512]{1,0:T(8,128)}, f32[128,512]{1,0:T(8,128)}) custom-call(f32[264,512]{1,0:T(8,128)} %get-tuple-element.18.d0, f32[264,512]{1,0:T(8,128)} %get-tuple-element.17.d3, f32[2,264,512]{2,1,0:T(8,128)} %bitcast.28, f32[2,264,512]{2,1,0:T(8,128)} %copy-done, f32[2,264,512]{2,1,0:T(8,128)} %get-tuple-element.21.aug), custom_call_target="tpu_custom_call" | custom-call | flops 104857600 | bytes 31457280 | tf_op jit(solution)/shard_map/inner_planes/pallas_call | solution.py:431
  91.1 0.0 collective-permute-done.below
  91.1 0.0 copy-start.1
  91.1 0.0 collective-permute-done.1.above
  91.1 0.0 copy-start.2
  91.1 0.8 copy-done.1
  91.9 0.2 copy-done.2
  92.1 6.9 %outer_planes.1 = f32[8,128,512]{2,1,0:T(8,128)} custom-call(f32[264,512]{1,0:T(8,128)} %copy-done.1, f32[264,512]{1,0:T(8,128)} %get-tuple-element.18.d0, f32[264,512]{1,0:T(8,128)} %get-tuple-element.17.d3, f32[264,512]{1,0:T(8,128)} %copy-done.2, f32[8,128,512]{2,1,0:T(8,128)} %get-tuple-element.22.old_ref, ...), custom_call_target="tpu_custom_call", output_to_operand_aliasing={{}: (4, {})} | custom-call | flops 104857600 | bytes 31457280 | tf_op jit(solution)/shard_map/outer_planes/pallas_call | solution.py:498
Async XLA Ops:
  41.2 38.9 %collective-permute-start.2 = (f32[2,264,512]{2,1,0:T(8,128)}, f32[2,264,512]{2,1,0:T(8,128)S(1)}, u32[]{:S(2)}, u32[]{:S(2)}) collective-permute-start(f32[2,264,512]{2,1,0:T(8,128)} %bitcast.29), channel_id=1, source_target_pairs={{0,64},{64,0},{32,96},{96,32},{1,65},{65,1},{33,97},{97,33},{2,66}... | collective-permute-start | bytes 3244040 | tf_op jit(solution)/shard_map/ppermute | solution.py:544
  58.3 32.8 %collective-permute-start = (f32[264,512]{1,0:T(8,128)}, f32[264,512]{1,0:T(8,128)S(1)}, u32[]{:S(2)}, u32[]{:S(2)}) collective-permute-start(f32[264,512]{1,0:T(8,128)} %get-tuple-element.17.d3), channel_id=1, source_target_pairs={{0,1},{1,2},{2,3},{3,4},{4,5},{5,6},{6,7},{7,8},{8,9},{9,10},{10,1... | collective-permute-start | bytes 1622024 | tf_op jit(solution)/shard_map/ppermute | solution.py:547
  59.8 31.3 %collective-permute-start.1 = (f32[264,512]{1,0:T(8,128)}, f32[264,512]{1,0:T(8,128)S(1)}, u32[]{:S(2)}, u32[]{:S(2)}) collective-permute-start(f32[264,512]{1,0:T(8,128)} %get-tuple-element.18.d0), channel_id=1, source_target_pairs={{1,0},{2,1},{3,2},{4,3},{5,4},{6,5},{7,6},{8,7},{9,8},{10,9},{11,1... | collective-permute-start | bytes 1622024 | tf_op jit(solution)/shard_map/ppermute | solution.py:546
  80.1 1.0 copy-start
  91.1 0.8 copy-start.1
  91.1 1.0 copy-start.2

commit v3 on v2

--- a/solution.py
+++ b/solution.py
@@ -38,14 +38,13 @@
 MESH = pl.DeviceIdType.MESH
 STEP = 8
 ORDER = (0, 3, 1, 2)
-TILES = GROUP // 8 * 4
 
 
 def front_kernel(
-    weights, rows, lanes, beta, core, orb,
-    w_ref, outer_ref, near_ref, far_ref,
-    buf, picked, keep, send, recv, come, w_mine, w_core, w_come,
-    load_sem, swap_out, swap_in, far_out, far_in, w_out, w_in,
+    occupation, live, index, proj, core, orb,
+    d0_ref, d3_ref, mid_ref,
+    buf, picked, keep, send, recv, come, w_mine, w_core, w_come, rows_v, rows, beta, tile_of, row_of, vt,
+    rows_sem, load_sem, swap_out, swap_in, far_out, far_in, w_out, w_in,
 ):
     band = lax.axis_index("band")
     dom = lax.axis_index("dom")
@@ -72,8 +71,24 @@
     barrier = pltpu.get_barrier_semaphore()
     for partner in (mate, opposite):
         pl.semaphore_signal(barrier, inc=1, device_id=partner, device_id_type=MESH)
-    w0 = weights[0]
-    w1 = weights[1]
+    w0 = occupation[0].astype(f32) * 0.001
+    w1 = occupation[1].astype(f32) * 0.001
+
+    cell = index[...]
+    x = cell >> 18
+    y = (cell >> 9) & 511
+    c = (cell >> 7) & 3
+    rows_v[...] = ((x * 64 + (y >> 3)) * 4 + c) * 16 + (y & 7)
+    to_rows = pltpu.make_async_copy(rows_v, rows, rows_sem.at[0])
+    to_rows.start()
+    own = (y - 128 * band) & 511
+    g = x >> 1
+    tile = jnp.where(g == 0, 0, jnp.where(g == 3, 1, g + 1)) * 4 + c
+    pair = (x & 1) * 2
+    rim = tile * 8 + pair + jnp.where(own >= 510, own - 510, own - 124)
+    is_rim = (own >= 510) | (own < 130)
+    tile_of[...] = jnp.where(own < 128, tile, jnp.where(is_rim, 16, -1))
+    row_of[...] = jnp.where(own < 128, (x & 1) * 128 + own, rim).astype(f32)
 
     def squares(tile, count):
         a = buf[pl.ds(tile, count), 0]
@@ -89,18 +104,18 @@
                 value = squares(x * 256 + q * 64 + 16 * j, 16)
                 if near and mine:
                     value = value + core[x, pl.ds(16 * j, 16)]
-                ref[near, gi, pl.ds(64 * i + 16 * j, 16)] = value
+                ref[near, gi, pl.ds(16 * i + 4 * j, 4)] = value.reshape(4, 4, 8, 128)
                 return 0
 
             lax.fori_loop(0, 4, body, 0)
             q_low = lax.rem(q + 3, 4)
             own = jnp.where(q_low == band, 1.0, 0.0)
             value = squares(x * 256 + q_low * 64 + 60, 4) + own * core[x, 60:64]
-            ref[near, gi, 128:132, 2 * i : 2 * i + 2, :] = value[:, 6:8, :]
+            ref[near, gi, 32, :, 2 * i : 2 * i + 2, :] = value[:, 6:8, :]
             q_high = lax.rem(q + 1, 4)
             own = jnp.where(q_high == band, 1.0, 0.0)
             value = squares(x * 256 + q_high * 64, 4) + own * core[x, 0:4]
-            ref[near, gi, 128:132, 4 + 2 * i : 6 + 2 * i, :] = value[:, 0:2, :]
+            ref[near, gi, 32, :, 4 + 2 * i : 6 + 2 * i, :] = value[:, 0:2, :]
 
     def swap(near, gi):
         return pltpu.make_async_remote_copy(
@@ -112,23 +127,24 @@
             device_id_type=MESH,
         )
 
-    def across(gi):
+    def across(gi, half):
+        part = pl.ds(0, 16) if half == 0 else pl.ds(16, 17)
         return pltpu.make_async_remote_copy(
-            src_ref=keep.at[0, gi],
-            dst_ref=come.at[gi],
-            send_sem=far_out.at[gi],
-            recv_sem=far_in.at[gi],
+            src_ref=keep.at[0, gi, part],
+            dst_ref=come.at[gi, part],
+            send_sem=far_out.at[2 * gi + half],
+            recv_sem=far_in.at[2 * gi + half],
             device_id=opposite,
             device_id_type=MESH,
         )
 
-    def summed(near, gi, put):
+    def add_received(near, gi):
         def body(j, _):
-            here = pl.ds(12 * j, 12)
-            put(here, keep[near, gi, here] + recv[near, gi, here])
+            here = pl.ds(3 * j, 3)
+            keep[near, gi, here] = keep[near, gi, here] + recv[near, gi, here]
             return 0
 
-        lax.fori_loop(0, TILES // 12, body, 0)
+        lax.fori_loop(0, 11, body, 0)
 
     for gi in range(4):
         for copy in loads(gi):
@@ -145,16 +161,11 @@
         swap(1, gi).start()
         fill(keep, gi, 1, True)
         swap(0, gi).wait()
-
-        def put_far(here, value):
-            keep[0, gi, here] = value
-
-        def put_out(here, value):
-            far_ref[gi - 2, here] = value
-
-        summed(0, gi, put_far if gi < 2 else put_out)
+        add_received(0, gi)
         if gi < 2:
-            across(gi).start()
+            across(gi, 0).start()
+        if gi < 1:
+            across(gi, 1).start()
 
     flat = buf.reshape(32768, 128)
     sub = lax.broadcasted_iota(i32, (128, 128), 0)
@@ -162,20 +173,22 @@
     even = two == 0
     odd = two == 1
     lane_ids = lax.broadcasted_iota(i32, (8, 128), 1)
-
-    def step(i, total):
+    to_rows.wait()
+
+    def gather_step(i, total):
         for j in range(STEP):
             for k in range(128):
                 r = rows[STEP * i + j, k]
                 picked[pl.ds(256 * j + 2 * k, 2), :] = flat[pl.ds(r, 2, stride=8), :]
         for j in range(STEP):
             b = STEP * i + j
-            hot = jnp.where(lanes[pl.ds(b, 1), :] == sub, 1.0, 0.0).astype(bf16)
+            hot = jnp.where((index[pl.ds(b, 1), :] & 127) == sub, 1.0, 0.0).astype(bf16)
             g = picked[256 * j : 256 * j + 256]
             g1 = g.astype(bf16)
             g2 = (g - g1.astype(f32)).astype(bf16)
             t = jnp.dot(g1, hot, preferred_element_type=f32) + jnp.dot(g2, hot, preferred_element_type=f32)
-            be = beta[b]
+            be = jnp.where(lane_ids < live[b], proj[b], 0.0)
+            beta[b] = be
             p0 = jnp.sum(jnp.where(even, t, 0.0), axis=0, keepdims=True)
             p1 = jnp.sum(jnp.where(odd, t, 0.0), axis=0, keepdims=True)
             c0 = jnp.sum(be * p0, axis=1, keepdims=True)
@@ -183,74 +196,119 @@
             total = jnp.where(lane_ids == b, w0 * c0 * c0 + w1 * c1 * c1, total)
         return total
 
-    w_mine[...] = lax.fori_loop(0, 64 // STEP, step, jnp.zeros((8, 128), f32))
-
-    def send_w(src, dst, at, target):
+    w_mine[...] = lax.fori_loop(0, 64 // STEP, gather_step, jnp.zeros((8, 128), f32))
+
+    def send_w(src, at, target):
         return pltpu.make_async_remote_copy(
             src_ref=src,
-            dst_ref=dst,
+            dst_ref=w_come.at[at],
             send_sem=w_out.at[at],
             recv_sem=w_in.at[at],
             device_id=target,
             device_id_type=MESH,
         )
 
-    first = send_w(w_mine, w_come.at[0], 0, mate)
+    first = send_w(w_mine, 0, mate)
     first.start()
-    for gi in range(4):
+    for gi in range(2):
         swap(1, gi).wait()
-
-        def put_near(here, value):
-            near_ref[gi - 2, here] = value
-
-        def put_keep(here, value):
-            keep[1, gi, here] = value
-
-        summed(1, gi, put_keep if gi < 2 else put_near)
+        add_received(1, gi)
     first.wait()
     w_core[...] = w_mine[...] + w_come[0]
-    second = send_w(w_core, w_come.at[1], 1, opposite)
+    second = send_w(w_core, 1, opposite)
     second.start()
-    for gi in range(2):
-        across(gi).wait()
-
-        def body(j, _):
-            here = pl.ds(12 * j, 12)
-            outer_ref[gi, here] = keep[1, gi, here] + come[gi, here]
+    across(1, 1).start()
+    for gi in range(2, 4):
+        for half in range(2):
+            across(gi, half).start()
+    for gi in range(2, 4):
+        swap(1, gi).wait()
+        add_received(1, gi)
+    second.wait()
+    strengths = w_core[...] + w_come[1]
+
+    def spread_step(b, _):
+        be = beta[b]
+        w = jnp.sum(jnp.where(lane_ids == b, strengths, 0.0), axis=1, keepdims=True)
+        at = jnp.sum(w * be * be, axis=0, keepdims=True)
+        a1 = at.astype(bf16).astype(f32)
+        hot = (index[pl.ds(b, 1), :] & 127) == sub
+        here = pl.ds(pl.multiple_of(128 * b, 128), 128)
+        vt[0:128, here] = jnp.where(hot, a1, 0.0).astype(bf16)
+        vt[128:256, here] = jnp.where(hot, at - a1, 0.0).astype(bf16)
+        return 0
+
+    lax.fori_loop(0, 64, spread_step, 0)
+
+    def spread_tile(t, count):
+        ids = lax.broadcasted_iota(i32, (count, 128), 0).astype(f32).astype(bf16)
+        acc = jnp.zeros((count, 256), f32)
+        for q in range(8):
+            hots = []
+            for b in range(8 * q, 8 * q + 8):
+                at = jnp.where(tile_of[b : b + 1, :] == t, row_of[b : b + 1, :], -1.0).astype(bf16)
+                hots.append(jnp.where(at == ids, jnp.ones((), bf16), jnp.zeros((), bf16)))
+            acc = acc + lax.dot_general(
+                jnp.concatenate(hots, axis=1),
+                vt[:, 1024 * q : 1024 * q + 1024],
+                NT,
+                preferred_element_type=f32,
+            )
+        return acc[:, :128] + acc[:, 128:]
+
+    rim_rows = spread_tile(16, 128)
+    picked[0:128, :] = rim_rows
+    for gi in range(4):
+        across(gi, 0).wait()
+        across(gi, 1).wait()
+        out = d0_ref if gi == 0 else d3_ref if gi == 1 else mid_ref.at[gi - 2]
+
+        def columns(c, _):
+            cols = pl.ds(pl.multiple_of(128 * c, 128), 128)
+            sums = keep[1, gi, pl.ds(0, 33), c] + come[gi, pl.ds(0, 33), c]
+            out[0:256, cols] = spread_tile(4 * gi + c, 256) + sums[0:32].reshape(256, 128)
+            rim = picked[pl.ds(pl.multiple_of((4 * gi + c) * 8, 8), 8), :]
+            out[256:264, cols] = rim + sums[32]
             return 0
 
-        lax.fori_loop(0, TILES // 12, body, 0)
-    second.wait()
-    w_ref[...] = w_core[...] + w_come[1]
-
-
-def front(weights, rows, lanes, beta, core, orbitals):
+        lax.fori_loop(0, 4, columns, 0)
+
+
+def front(occupation, live, index, proj, core, orbitals):
     tiles = orbitals.reshape(2, 8, 64, 8, 4, 128).transpose(0, 1, 2, 4, 3, 5).reshape(2, 8, 256, 8, 128)
     core = core.reshape(8, 16, 8, 4, 128).transpose(0, 1, 3, 2, 4).reshape(8, 64, 8, 128)
-    pair = jax.ShapeDtypeStruct((2, TILES, 8, 128), f32)
-    both = pltpu.VMEM((2, 4, TILES, 8, 128), f32)
+    group = jax.ShapeDtypeStruct((GROUP, 512), f32)
+    both = pltpu.VMEM((2, 4, 33, 4, 8, 128), f32)
     strengths = pltpu.VMEM((8, 128), f32)
+    points = pltpu.VMEM((64, 128), i32)
     dma = pltpu.SemaphoreType.DMA
-    w, outer_sum, near, far = pl.pallas_call(
+    return pl.pallas_call(
         front_kernel,
         in_specs=[SM, SM, VM, VM, VM, HBM],
-        out_specs=[VM] * 4,
-        out_shape=[jax.ShapeDtypeStruct((8, 128), f32), pair, pair, pair],
+        out_specs=[VM] * 3,
+        out_shape=[group, group, jax.ShapeDtypeStruct((2, GROUP, 512), f32)],
         scratch_shapes=[
             pltpu.VMEM((2048, 2, 8, 128), f32),
             pltpu.VMEM((256 * STEP, 128), f32),
             both,
             both,
             both,
-            pltpu.VMEM((2, TILES, 8, 128), f32),
+            pltpu.VMEM((4, 33, 4, 8, 128), f32),
             strengths,
             strengths,
             pltpu.VMEM((2, 8, 128), f32),
+            points,
+            pltpu.SMEM((64, 128), i32),
+            pltpu.VMEM((64, 8, 128), f32),
+            points,
+            pltpu.VMEM((64, 128), f32),
+            pltpu.VMEM((256, 8192), bf16),
+            dma((1,)),
             dma((16,)),
             dma((8,)),
             dma((8,)),
-            dma((2,)),
-            dma((2,)),
+            dma((8,)),
+            dma((8,)),
             dma((2,)),
             dma((2,)),
         ],
@@ -259,85 +317,7 @@
         ),
         cost_estimate=pl.CostEstimate(flops=100 * MIB, bytes_accessed=40 * MIB, transcendentals=0),
         name="front",
-    )(weights, rows, lanes, beta, core, tiles)
-    plain = lambda t: t.reshape(2, 33, 4, 8, 128).transpose(0, 1, 3, 2, 4).reshape(2, GROUP, 512)
-    return w, plain(outer_sum), plain(near), plain(far)
-
-
-def scatter_kernel(
-    rows, lanes, beta, strength_ref, sums, d0_ref, d3_ref, aug_ref, spread, *accs
-):
-    for acc in accs:
-        acc[...] = jnp.zeros_like(acc)
-    strengths = strength_ref[...]
-    sub = lax.broadcasted_iota(i32, (128, 128), 0)
-    eye = sub == lax.broadcasted_iota(i32, (128, 128), 1)
-    lane_ids = lax.broadcasted_iota(i32, (8, 128), 1)
-
-    def spread_step(i, _):
-        for j in range(STEP):
-            b = STEP * i + j
-            be = beta[b]
-            w = jnp.sum(jnp.where(lane_ids == b, strengths, 0.0), axis=1, keepdims=True)
-            at = jnp.sum(w * be * be, axis=0, keepdims=True)
-            a1 = at.astype(bf16).astype(f32)
-            hot = jnp.where(lanes[pl.ds(b, 1), :] == sub, 1.0, 0.0).astype(bf16)
-            d1 = jnp.where(eye, a1, 0.0).astype(bf16)
-            d2 = jnp.where(eye, at - a1, 0.0).astype(bf16)
-            spread[pl.ds(pl.multiple_of(b * 128, 128), 128), :] = lax.dot_general(
-                d1, hot, NT, preferred_element_type=f32
-            ) + lax.dot_general(d2, hot, NT, preferred_element_type=f32)
-        return 0
-
-    lax.fori_loop(0, 64 // STEP, spread_step, 0)
-
-    def add_step(b, _):
-        first = pl.multiple_of(b * 128, 128)
-        for k in range(0, 128, N_ACC):
-            at_rows = [rows[b, k + j] for j in range(N_ACC)]
-            old = [accs[j][pl.ds(at_rows[j], 1), :] for j in range(N_ACC)]
-            for j in range(N_ACC):
-                accs[j][pl.ds(at_rows[j], 1), :] = old[j] + spread[pl.ds(first + k + j, 1), :]
-        return 0
-
-    lax.fori_loop(0, 64, add_step, 0)
-
-    def summed(g, c):
-        piece = pl.ds((g * 4 + c) * GROUP, GROUP)
-        total = accs[0][piece, :]
-        for acc in accs[1:]:
-            total = total + acc[piece, :]
-        return total
-
-    for at, g, ref in ((0, 0, d0_ref), (1, 3, d3_ref)):
-        for c in range(4):
-            cols = slice(128 * c, 128 * c + 128)
-            ref[:, cols] = sums[at, :, cols] + summed(g, c)
-    for at, g in ((0, 1), (1, 2)):
-        for c in range(4):
-            aug_ref[at, :, 128 * c : 128 * c + 128] = summed(g, c)
-
-
-def scatter(rows, lanes, beta, strengths, sums):
-    group = jax.ShapeDtypeStruct((GROUP, 512), f32)
-    whole2 = lambda *shape: pl.BlockSpec(shape, lambda s: (0,) * len(shape))
-    return pl.pallas_call(
-        scatter_kernel,
-        grid=(1,),
-        in_specs=[
-            SM,
-            whole2(64, 128),
-            whole2(64, 8, 128),
-            whole2(8, 128),
-            whole2(2, GROUP, 512),
-        ],
-        out_specs=[whole2(GROUP, 512), whole2(GROUP, 512), whole2(2, GROUP, 512)],
-        out_shape=[group, group, jax.ShapeDtypeStruct((2, GROUP, 512), f32)],
-        scratch_shapes=[pltpu.VMEM((8192, 128), f32)] + [pltpu.VMEM((ACC_ROWS + 8, 128), f32)] * N_ACC,
-        compiler_params=params(60),
-        cost_estimate=pl.CostEstimate(flops=100 * MIB, bytes_accessed=80 * MIB, transcendentals=0),
-        name="scatter_points",
-    )(rows, lanes, beta, strengths, sums)
+    )(occupation, live, index, proj, core, tiles)
 
 
 def place_group(dens, plane, group, lead=None):
@@ -385,15 +365,11 @@
     return (up - down) * 0.5
 
 
-def inner_kernel(d0, d3, near, far, aug, pot_ref, low_ref, high_ref, dens, flux_x, flux_y):
+def inner_kernel(d0, d3, mid, pot_ref, low_ref, high_ref, dens, flux_x, flux_y):
     place_group(dens, 0, d0)
     place_group(dens, 6, d3)
-    for g in range(2):
-        total = near[g] + far[g] + aug[g]
-        for i in range(2):
-            dens[2 + 2 * g + i, 16:144, :] = total[128 * i : 128 * i + 128]
-            dens[2 + 2 * g + i, 14:16, :] = total[LOW + 2 * i : LOW + 2 * i + 2]
-            dens[2 + 2 * g + i, 144:146, :] = total[HIGH + 2 * i : HIGH + 2 * i + 2]
+    place_group(dens, 2, mid.at[0])
+    place_group(dens, 4, mid.at[1])
 
     def plane(x, _):
         def put(row, value, fx):
@@ -425,13 +401,13 @@
     high_ref[...] = flux_x[6]
 
 
-def inner(d0, d3, near, far, aug):
+def inner(d0, d3, mid):
     whole2 = lambda *shape: pl.BlockSpec(shape, lambda s: (0,) * len(shape))
     plane = jax.ShapeDtypeStruct((128, 512), f32)
     return pl.pallas_call(
         inner_kernel,
         grid=(1,),
-        in_specs=[whole2(GROUP, 512)] * 2 + [whole2(2, GROUP, 512)] * 3,
+        in_specs=[whole2(GROUP, 512)] * 2 + [whole2(2, GROUP, 512)],
         out_specs=[whole2(8, 128, 512), whole2(128, 512), whole2(128, 512)],
         out_shape=[jax.ShapeDtypeStruct((8, 128, 512), f32), plane, plane],
         scratch_shapes=[
@@ -442,7 +418,7 @@
         compiler_params=params(60),
         cost_estimate=pl.CostEstimate(flops=100 * MIB, bytes_accessed=30 * MIB, transcendentals=0),
         name="inner_planes",
-    )(d0, d3, near, far, aug)
+    )(d0, d3, mid)
 
 
 def outer_kernel(below, d0, d3, above, old, low, high, pot_ref, dens, flux_x, flux_y):
@@ -516,36 +492,12 @@
 
 
 def shards(orbitals, occupation, core_density, proj_values, block_index, live_points):
-    band = lax.axis_index("band")
-    weights = occupation.astype(f32) * 0.001
-    far_pairs = [(0, 2), (2, 0), (1, 3), (3, 1)]
-
-    point_ids = lax.broadcasted_iota(i32, block_index.shape, 1)
-    beta = proj_values * (point_ids < live_points[:, None]).astype(f32)[:, None, :]
-    x = block_index >> 18
-    y = (block_index >> 9) & 511
-    c = (block_index >> 7) & 3
-    lanes = block_index & 127
-    from_rows = ((x * 64 + (y >> 3)) * 4 + c) * 16 + (y & 7)
-    own = (y - 128 * band) & 511
-    pair = (x & 1) * 2
-    inside = jnp.where(
-        own < 128,
-        (x & 1) * 128 + own,
-        jnp.where(own >= 510, LOW + pair + own - 510, HIGH + pair + own - 128),
+    d0, d3, mid = front(
+        occupation, live_points, block_index, proj_values, core_density, orbitals
     )
-    into_rows = jnp.where(
-        (own < 130) | (own >= 510), ((x >> 1) * 4 + c) * GROUP + inside, ACC_ROWS
-    )
-
-    strengths, outer_sum, near, far = front(
-        weights, from_rows, lanes, beta, core_density, orbitals
-    )
-    far = lax.ppermute(far, "band", far_pairs)
-    d0, d3, aug = scatter(into_rows, lanes, beta, strengths, outer_sum)
     above = lax.ppermute(d0, "dom", [((i + 1) % 32, i) for i in range(32)])
     below = lax.ppermute(d3, "dom", [(i, (i + 1) % 32) for i in range(32)])
-    part, low, high = inner(d0, d3, near, far, aug)
+    part, low, high = inner(d0, d3, mid)
     return outer(below, d0, d3, above, part, low, high)
 
 

time: 99.3 us -> 92.9 us (0.936)
  Pallas kernels: 68.8 us -> 82.2 us
  waiting for transfers between devices: 15.6 us -> 2.97 us
  other arithmetic: 5 us -> 0 us
  starting transfers between devices: 7.56 us -> 6.31 us
    pallas_call x1, Pallas kernels: 36.2 us -> 66 us  [front(): pl.pallas_call(front_kernel, in_specs=[SM, SM, VM, VM, VM, HBM], out_spec...]
    pallas_call x1 -> x0, Pallas kernels: 15.8 us -> none  [scatter(): pl.pallas_call(scatter_kernel, grid=(1,), in_specs=[SM, whole2(64, 128),...]
    ppermute x1 -> x0, waiting for transfers between devices: 15.6 us -> none  [shards(): far = lax.ppermute(far, 'band', far_pairs)]
    ppermute x1, waiting for transfers between devices: 0.01 us -> 2.97 us  [shards(): below = lax.ppermute(d3, 'dom', [(i, (i + 1) % 32) for i in range(32)])]
    mul x2 -> x0, other arithmetic: 2.84 us -> none  [the longest x1 1.68 us: shards(): proj_values * (point_ids < live_points[:, None]).astype(f32)[:, None, :]]
    add x1 -> x0, other arithmetic: 1.43 us -> none  [shards(): from_rows = ((x * 64 + (y >> 3)) * 4 + c) * 16 + (y & 7)]
    ppermute x1 -> x0, starting transfers between devices: 1.32 us -> none  [shards(): far = lax.ppermute(far, 'band', far_pairs)]
  transfers between devices with their start and end apart: 3 -> 2, of which waited for: 1 -> 1; matrix products, arithmetic and copies ran while one was open for 0% -> 0% of each run, Pallas kernels for 26% -> 10%
where the time goes in v3:
time: 92.9 us; the launch traced here: 92.6 us
  Pallas kernels  82.2 us (88%)
  starting transfers between devices  6.31 us (7%)
  waiting for transfers between devices  2.97 us (3%)
  local copies, waits for them, and re-layouts  0.97 us (1%)
    pallas_call x1, Pallas kernels, front(): pl.pallas_call(front_kernel, in_specs=[SM, SM, VM, VM, VM, HBM], out_spec...  66 us
    pallas_call x1, Pallas kernels, inner(): pl.pallas_call(inner_kernel, grid=(1,), in_specs=[whole2(GROUP, 512)] * 2...  9.25 us
    pallas_call x1, Pallas kernels, outer(): pl.pallas_call(outer_body, in_specs=[VM, VM, VM, VM, ANY, VM, VM], out_sp...  6.88 us
    ppermute x1, starting transfers between devices, shards(): above = lax.ppermute(d0, 'dom', [((i + 1) % 32, i) for i in range(32)])  4.75 us
    ppermute x1, waiting for transfers between devices, shards(): below = lax.ppermute(d3, 'dom', [(i, (i + 1) % 32) for i in range(32)])  2.97 us
  transfers between devices with their start and end apart: 2, of which 1 were waited for; matrix products, arithmetic and copies ran while one was open for 0% of the time, Pallas kernels for 10%

profile of v3, /device:TPU:0, one launch (start us, length us, event | category | flops | bytes accessed | tf_op | source)
XLA Modules:
  0.0 92.6 jit_solution(7865796759322511506)
XLA Ops:
  0.0 66.0 %front.1 = (f32[264,512]{1,0:T(8,128)}, f32[264,512]{1,0:T(8,128)}, f32[2,264,512]{2,1,0:T(8,128)}) custom-call(s32[2]{0:T(128)} %occupation.1, s32[64]{0:T(128)} %live.1, s32[64,128]{1,0:T(8,128)} %index.1, f32[64,8,128]{2,1,0:T(8,128)} %proj.1, f32[8,64,8,128]{3,2,1,0:T(8,128)} %bitcast.11, f32[2,8,256,8,128]{4,3,2,1,0:T(8,128)} %bitcast.10), custom_call_target="tpu_custom_call" | custom-call | flops 104857600 | bytes 41943040 | tf_op jit(solution)/shard_map/front/pallas_call | solution.py:285
  66.0 1.6 %collective-permute-start = (f32[264,512]{1,0:T(8,128)}, f32[264,512]{1,0:T(8,128)S(1)}, u32[]{:S(2)}, u32[]{:S(2)}) collective-permute-start(f32[264,512]{1,0:T(8,128)} %get-tuple-element.11.d3), channel_id=1, source_target_pairs={{0,1},{1,2},{2,3},{3,4},{4,5},{5,6},{6,7},{7,8},{8,9},{9,10},{10,1... | collective-permute-start | bytes 1622024 | tf_op jit(solution)/shard_map/ppermute | solution.py:499
  67.6 4.7 %collective-permute-start.1 = (f32[264,512]{1,0:T(8,128)}, f32[264,512]{1,0:T(8,128)S(1)}, u32[]{:S(2)}, u32[]{:S(2)}) collective-permute-start(f32[264,512]{1,0:T(8,128)} %get-tuple-element.12.d0), channel_id=1, source_target_pairs={{1,0},{2,1},{3,2},{4,3},{5,4},{6,5},{7,6},{8,7},{9,8},{10,9},{11,1... | collective-permute-start | bytes 1622024 | tf_op jit(solution)/shard_map/ppermute | solution.py:498
  72.4 9.2 %inner_planes.1 = (f32[8,128,512]{2,1,0:T(8,128)}, f32[128,512]{1,0:T(8,128)}, f32[128,512]{1,0:T(8,128)}) custom-call(f32[264,512]{1,0:T(8,128)} %get-tuple-element.12.d0, f32[264,512]{1,0:T(8,128)} %get-tuple-element.11.d3, f32[2,264,512]{2,1,0:T(8,128)} %get-tuple-element.13.mid), custom_call_target="tpu_custom_call" | custom-call | flops 104857600 | bytes 31457280 | tf_op jit(solution)/shard_map/inner_planes/pallas_call | solution.py:407
  81.6 3.0 %collective-permute-done.below = f32[264,512]{1,0:T(8,128)S(1)} collective-permute-done((f32[264,512]{1,0:T(8,128)}, f32[264,512]{1,0:T(8,128)S(1)}, u32[]{:S(2)}, u32[]{:S(2)}) %collective-permute-start) | collective-permute-done | bytes 540704 | tf_op jit(solution)/shard_map/ppermute | solution.py:499
  84.6 0.0 copy-start
  84.6 0.0 collective-permute-done.1.above
  84.6 0.0 copy-start.1
  84.6 0.8 copy-done
  85.4 0.2 copy-done.1
  85.6 6.9 %outer_planes.1 = f32[8,128,512]{2,1,0:T(8,128)} custom-call(f32[264,512]{1,0:T(8,128)} %copy-done, f32[264,512]{1,0:T(8,128)} %get-tuple-element.12.d0, f32[264,512]{1,0:T(8,128)} %get-tuple-element.11.d3, f32[264,512]{1,0:T(8,128)} %copy-done.1, f32[8,128,512]{2,1,0:T(8,128)} %get-tuple-element.14.old_ref, ...), custom_call_target="tpu_custom_call", output_to_operand_aliasing={{}: (4, {})} | custom-call | flops 104857600 | bytes 31457280 | tf_op jit(solution)/shard_map/outer_planes/pallas_call | solution.py:474
Async XLA Ops:
  66.0 18.5 %collective-permute-start = (f32[264,512]{1,0:T(8,128)}, f32[264,512]{1,0:T(8,128)S(1)}, u32[]{:S(2)}, u32[]{:S(2)}) collective-permute-start(f32[264,512]{1,0:T(8,128)} %get-tuple-element.11.d3), channel_id=1, source_target_pairs={{0,1},{1,2},{2,3},{3,4},{4,5},{5,6},{6,7},{7,8},{8,9},{9,10},{10,1... | collective-permute-start | bytes 1622024 | tf_op jit(solution)/shard_map/ppermute | solution.py:499
  67.6 17.0 %collective-permute-start.1 = (f32[264,512]{1,0:T(8,128)}, f32[264,512]{1,0:T(8,128)S(1)}, u32[]{:S(2)}, u32[]{:S(2)}) collective-permute-start(f32[264,512]{1,0:T(8,128)} %get-tuple-element.12.d0), channel_id=1, source_target_pairs={{1,0},{2,1},{3,2},{4,3},{5,4},{6,5},{7,6},{8,7},{9,8},{10,9},{11,1... | collective-permute-start | bytes 1622024 | tf_op jit(solution)/shard_map/ppermute | solution.py:498
  84.6 0.8 copy-start
  84.6 1.0 %copy-start.1 = (f32[264,512]{1,0:T(8,128)}, f32[264,512]{1,0:T(8,128)S(1)}, u32[]{:S(2)}) copy-start(f32[264,512]{1,0:T(8,128)S(1)} %collective-permute-done.1.above) | copy-start | bytes 1622020

commit v4 on v3

v4 whole, which is shorter than its diff:
```python
import functools
import math

import jax
import jax.numpy as jnp
from jax import lax
from jax.experimental import pallas as pl
from jax.experimental.pallas import tpu as pltpu
from jax.sharding import PartitionSpec as P

f32 = jnp.float32
bf16 = jnp.bfloat16
i32 = jnp.int32

coef_a = 0.75 * (3.0 / math.pi) ** (1.0 / 3.0)
kappa_val = 0.804
mu_val = 0.2195149727645171
s_scale = 4.0 * (3.0 * math.pi**2) ** (2.0 / 3.0)
LOG2E = math.log2(math.e)

MIB = 2**20
GROUP = 264
LOW = 256
HIGH = 260
ACC_ROWS = 16 * GROUP
N_ACC = 8
NT = (((1,), (1,)), ((), ()))
VM = pl.BlockSpec(memory_space=pltpu.VMEM)
SM = pl.BlockSpec(memory_space=pltpu.SMEM)
ANY = pl.BlockSpec(memory_space=pl.ANY)
HBM = pl.BlockSpec(memory_space=pltpu.HBM)


def params(mib):
    return pltpu.CompilerParams(vmem_limit_bytes=mib * MIB)


def local_parts(dens, x, row, count):
    mid = dens[x, pl.ds(row, count), :]
    gy = (dens[x, pl.ds(row + 1, count), :] - dens[x, pl.ds(row - 1, count), :]) * 0.5
    gx = (dens[x + 1, pl.ds(row, count), :] - dens[x - 1, pl.ds(row, count), :]) * 0.5
    gz = (pltpu.roll(mid, 511, 1) - pltpu.roll(mid, 1, 1)) * 0.5
    sigma = gy * gy + gx * gx + gz * gz
    logs = jnp.log(mid)
    cube = jnp.exp2(logs * (LOG2E / 3.0))
    inv_four = jnp.exp2(logs * (-4.0 * LOG2E / 3.0))
    reduced = sigma * (inv_four * inv_four) * (1.0 / s_scale)
    under = 1.0 + (mu_val / kappa_val) * reduced
    inv = pl.reciprocal(under, approx=True)
    inv = inv * (2.0 - under * inv)
    slope = mu_val * inv * inv
    factor = (1.0 + kappa_val) - kappa_val * inv
    e_n = (-4.0 / 3.0 * coef_a) * cube * (factor - 2.0 * reduced * slope)
    twice = (-2.0 * coef_a / s_scale) * inv_four * slope
    return e_n, twice * gy, twice * gx, twice * gz


STRIP = 16


def full_plane(dens, x, flux_y, put):
    for row in (8, 144):
        flux_y[pl.ds(row, 8), :] = local_parts(dens, x, row, 8)[1]
    for row in range(16, 144, STRIP):
        e_n, fy, fx, fz = local_parts(dens, x, row, STRIP)
        flux_y[pl.ds(row, STRIP), :] = fy
        put(row - 16, e_n - (pltpu.roll(fz, 511, 1) - pltpu.roll(fz, 1, 1)) * 0.5, fx)


def minus_y(flux_y, row):
    up = flux_y[pl.ds(row + 17, STRIP), :]
    down = flux_y[pl.ds(row + 15, STRIP), :]
    return (up - down) * 0.5


MESH = pl.DeviceIdType.MESH
STEP = 8
ORDER = (0, 3, 1, 2)


def potential_kernel(
    occupation, live, index, proj, core, orb,
    pot_ref,
    buf, picked_a, picked_b, rims, dens, flux_x, flux_y, keep, send, recv, come, w_mine, w_core, w_come, rows_v, rows, beta, tile_of, row_of, vt,
    rows_sem, load_sem, swap_out, swap_in, far_out, far_in, w_out, w_in, halo_out, halo_in,
):
    band = lax.axis_index("band")
    dom = lax.axis_index("dom")
    parity = lax.rem(band, 2)
    z_hi = band // 2
    mate = (band + 1 - 2 * parity, dom)
    opposite = (lax.rem(band + 2, 4), dom)
    after = (band, lax.rem(dom + 1, 32))
    before = (band, lax.rem(dom + 31, 32))

    def loads(gi):
        made = []
        for i in range(2):
            x = 2 * ORDER[gi] + i
            for o in range(2):
                made.append(
                    pltpu.make_async_copy(
                        orb.at[o, x], buf.at[pl.ds(256 * x, 256), o], load_sem.at[4 * gi + 2 * i + o]
                    )
                )
        return made

    for gi in range(2):
        for copy in loads(gi):
            copy.start()
    barrier = pltpu.get_barrier_semaphore()
    for partner in (mate, opposite, after, before):
        pl.semaphore_signal(barrier, inc=1, device_id=partner, device_id_type=MESH)
    w0 = occupation[0].astype(f32) * 0.001
    w1 = occupation[1].astype(f32) * 0.001

    cell = index[...]
    x = cell >> 18
    y = (cell >> 9) & 511
    c = (cell >> 7) & 3
    rows_v[...] = ((x * 64 + (y >> 3)) * 4 + c) * 16 + (y & 7)
    to_rows = pltpu.make_async_copy(rows_v, rows, rows_sem.at[0])
    to_rows.start()
    own = (y - 128 * band) & 511
    g = x >> 1
    tile = jnp.where(g == 0, 0, jnp.where(g == 3, 1, g + 1)) * 4 + c
    pair = (x & 1) * 2
    rim = tile * 8 + pair + jnp.where(own >= 510, own - 510, own - 124)
    is_rim = (own >= 510) | (own < 130)
    tile_of[...] = jnp.where(own < 128, tile, jnp.where(is_rim, 16, -1))
    row_of[...] = jnp.where(own < 128, (x & 1) * 128 + own, rim).astype(f32)

    def squares(tile, count):
        a = buf[pl.ds(tile, count), 0]
        b = buf[pl.ds(tile, count), 1]
        return w0 * a * a + w1 * b * b

    def fill(ref, gi, near, mine):
        q = 2 * (z_hi if near else 1 - z_hi) + (parity if mine else 1 - parity)
        for i in range(2):
            x = 2 * ORDER[gi] + i

            def body(j, _):
                value = squares(x * 256 + q * 64 + 16 * j, 16)
                if near and mine:
                    value = value + core[x, pl.ds(16 * j, 16)]
                ref[near, gi, pl.ds(16 * i + 4 * j, 4)] = value.reshape(4, 4, 8, 128)
                return 0

            lax.fori_loop(0, 4, body, 0, unroll=2)
            q_low = lax.rem(q + 3, 4)
            own = jnp.where(q_low == band, 1.0, 0.0)
            value = squares(x * 256 + q_low * 64 + 60, 4) + own * core[x, 60:64]
            ref[near, gi, 32, :, 2 * i : 2 * i + 2, :] = value[:, 6:8, :]
            q_high = lax.rem(q + 1, 4)
            own = jnp.where(q_high == band, 1.0, 0.0)
            value = squares(x * 256 + q_high * 64, 4) + own * core[x, 0:4]
            ref[near, gi, 32, :, 4 + 2 * i : 6 + 2 * i, :] = value[:, 0:2, :]

    def swap(near, gi):
        return pltpu.make_async_remote_copy(
            src_ref=send.at[near, gi],
            dst_ref=recv.at[near, gi],
            send_sem=swap_out.at[4 * near + gi],
            recv_sem=swap_in.at[4 * near + gi],
            device_id=mate,
            device_id_type=MESH,
        )

    def across(gi, half):
        part = pl.ds(0, 16) if half == 0 else pl.ds(16, 17)
        return pltpu.make_async_remote_copy(
            src_ref=keep.at[0, gi, part],
            dst_ref=come.at[gi, part],
            send_sem=far_out.at[2 * gi + half],
            recv_sem=far_in.at[2 * gi + half],
            device_id=opposite,
            device_id_type=MESH,
        )

    def add_received(near, gi):
        def body(j, _):
            here = pl.ds(3 * j, 3)
            keep[near, gi, here] = keep[near, gi, here] + recv[near, gi, here]
            return 0

        lax.fori_loop(0, 11, body, 0)

    for gi in range(4):
        for copy in loads(gi):
            copy.wait()
        if gi < 2:
            for copy in loads(gi + 2):
                copy.start()
        fill(send, gi, 0, False)
        if gi == 0:
            pl.semaphore_wait(barrier, 4)
        swap(0, gi).start()
        fill(keep, gi, 0, True)
        fill(send, gi, 1, False)
        swap(1, gi).start()
        fill(keep, gi, 1, True)
        swap(0, gi).wait()
        add_received(0, gi)
        if gi < 2:
            across(gi, 0).start()
        if gi < 1:
            across(gi, 1).start()

    flat = buf.reshape(32768, 128)
    sub = lax.broadcasted_iota(i32, (128, 128), 0)
    two = lax.broadcasted_iota(i32, (256, 128), 0) - 2 * lax.broadcasted_iota(i32, (256, 128), 1)
    even = two == 0
    odd = two == 1
    lane_ids = lax.broadcasted_iota(i32, (8, 128), 1)
    to_rows.wait()

    def pick(step, j, picked):
        for k in range(128):
            r = rows[STEP * step + j, k]
            picked[pl.ds(256 * j + 2 * k, 2), :] = flat[pl.ds(r, 2, stride=8), :]

    def project(step, j, picked, total):
        b = STEP * step + j
        hot = jnp.where((index[pl.ds(b, 1), :] & 127) == sub, 1.0, 0.0).astype(bf16)
        g = picked[256 * j : 256 * j + 256]
        g1 = g.astype(bf16)
        g2 = (g - g1.astype(f32)).astype(bf16)
        t = jnp.dot(g1, hot, preferred_element_type=f32) + jnp.dot(g2, hot, preferred_element_type=f32)
        be = jnp.where(lane_ids < live[b], proj[b], 0.0)
        beta[b] = be
        p0 = jnp.sum(jnp.where(even, t, 0.0), axis=0, keepdims=True)
        p1 = jnp.sum(jnp.where(odd, t, 0.0), axis=0, keepdims=True)
        c0 = jnp.sum(be * p0, axis=1, keepdims=True)
        c1 = jnp.sum(be * p1, axis=1, keepdims=True)
        return jnp.where(lane_ids == b, w0 * c0 * c0 + w1 * c1 * c1, total)

    def gather_step(i, total):
        for j in range(STEP):
            pick(2 * i + 1, j, picked_b)
            total = project(2 * i, j, picked_a, total)
        for j in range(STEP):
            pick(jnp.minimum(2 * i + 2, 64 // STEP - 1), j, picked_a)
            total = project(2 * i + 1, j, picked_b, total)
        return total

    for j in range(STEP):
        pick(0, j, picked_a)
    w_mine[...] = lax.fori_loop(0, 32 // STEP, gather_step, jnp.zeros((8, 128), f32))

    def send_w(src, at, target):
        return pltpu.make_async_remote_copy(
            src_ref=src,
            dst_ref=w_come.at[at],
            send_sem=w_out.at[at],
            recv_sem=w_in.at[at],
            device_id=target,
            device_id_type=MESH,
        )

    first = send_w(w_mine, 0, mate)
    first.start()
    for gi in range(2):
        swap(1, gi).wait()
        add_received(1, gi)
    first.wait()
    w_core[...] = w_mine[...] + w_come[0]
    second = send_w(w_core, 1, opposite)
    second.start()
    across(1, 1).start()
    for gi in range(2, 4):
        for half in range(2):
            across(gi, half).start()
    for gi in range(2, 4):
        swap(1, gi).wait()
        add_received(1, gi)
    second.wait()
    strengths = w_core[...] + w_come[1]

    def spread_step(i, _):
        for j in range(STEP):
            b = STEP * i + j
            be = beta[b]
            w = jnp.sum(jnp.where(lane_ids == b, strengths, 0.0), axis=1, keepdims=True)
            at = jnp.sum(w * be * be, axis=0, keepdims=True)
            a1 = at.astype(bf16).astype(f32)
            hot = (index[pl.ds(b, 1), :] & 127) == sub
            here = pl.ds(pl.multiple_of(128 * STEP * i, 128 * STEP) + 128 * j, 128)
            vt[0:128, here] = jnp.where(hot, a1, 0.0).astype(bf16)
            vt[128:256, here] = jnp.where(hot, at - a1, 0.0).astype(bf16)
        return 0

    lax.fori_loop(0, 64 // STEP, spread_step, 0)

    def spread_tile(t, count):
        ids = lax.broadcasted_iota(i32, (count, 128), 0).astype(f32).astype(bf16)
        acc = jnp.zeros((count, 256), f32)
        for q in range(8):
            hots = []
            for b in range(8 * q, 8 * q + 8):
                at = jnp.where(tile_of[b : b + 1, :] == t, row_of[b : b + 1, :], -1.0).astype(bf16)
                hots.append(jnp.where(at == ids, jnp.ones((), bf16), jnp.zeros((), bf16)))
            acc = acc + lax.dot_general(
                jnp.concatenate(hots, axis=1),
                vt[:, 1024 * q : 1024 * q + 1024],
                NT,
                preferred_element_type=f32,
            )
        return acc[:, :128] + acc[:, 128:]

    rims[...] = spread_tile(16, 128)

    def density(gi, arrived):
        at = 2 + 2 * ORDER[gi]

        def columns(c, _):
            cols = pl.ds(pl.multiple_of(128 * c, 128), 128)
            sums = keep[1, gi, pl.ds(0, 33), c]
            if arrived:
                sums = sums + come[gi, pl.ds(0, 33), c]
            body = spread_tile(4 * gi + c, 256) + sums[0:32].reshape(256, 128)
            rim = rims[pl.ds(pl.multiple_of((4 * gi + c) * 8, 8), 8), :] + sums[32]
            for i in range(2):
                dens[at + i, 16:144, cols] = body[128 * i : 128 * i + 128]
                dens[at + i, 14:16, cols] = rim[2 * i : 2 * i + 2]
                dens[at + i, 144:146, cols] = rim[4 + 2 * i : 6 + 2 * i]
            return 0

        lax.fori_loop(0, 4, columns, 0)

    def add_arrived(gi):
        at = 2 + 2 * ORDER[gi]

        def columns(c, _):
            cols = pl.ds(pl.multiple_of(128 * c, 128), 128)
            rim = come[gi, 32, c]
            for i in range(2):
                dens[at + i, 16:144, cols] = dens[at + i, 16:144, cols] + come[
                    gi, pl.ds(16 * i, 16), c
                ].reshape(128, 128)
                dens[at + i, 14:16, cols] = dens[at + i, 14:16, cols] + rim[2 * i : 2 * i + 2]
                dens[at + i, 144:146, cols] = dens[at + i, 144:146, cols] + rim[4 + 2 * i : 6 + 2 * i]
            return 0

        lax.fori_loop(0, 4, columns, 0)

    def halo(at, source, target, row, count, partner):
        return pltpu.make_async_remote_copy(
            src_ref=dens.at[source, pl.ds(row, count)],
            dst_ref=dens.at[target, pl.ds(row, count)],
            send_sem=halo_out.at[at],
            recv_sem=halo_in.at[at],
            device_id=partner,
            device_id_type=MESH,
        )

    def wait_far(gi):
        across(gi, 0).wait()
        across(gi, 1).wait()

    def plane(x, _):
        def put(row, value, fx):
            pot_ref[x, pl.ds(row, STRIP), :] = value
            flux_x[x + 1, pl.ds(row, STRIP), :] = fx

        full_plane(dens, x + 2, flux_y, put)
        for row in range(0, 128, STRIP):
            here = pl.ds(row, STRIP)
            pot_ref[x, here, :] = pot_ref[x, here, :] - minus_y(flux_y, row)
        return 0

    def along_x(x, _):
        for row in range(0, 128, STRIP):
            here = pl.ds(row, STRIP)
            pot_ref[x, here, :] = (
                pot_ref[x, here, :] - (flux_x[x + 2, here, :] - flux_x[x, here, :]) * 0.5
            )
        return 0

    wait_far(0)
    density(0, True)
    halos = [halo(0, 2, 10, 8, 144, before), halo(1, 3, 11, 16, 128, before)]
    for copy in halos:
        copy.start()
    wait_far(1)
    density(1, True)
    more = [halo(2, 9, 1, 8, 144, after), halo(3, 8, 0, 16, 128, after)]
    for copy in more:
        copy.start()
    wait_far(2)
    density(2, True)
    lax.fori_loop(1, 3, plane, 0)
    density(3, False)
    wait_far(3)
    add_arrived(3)
    lax.fori_loop(3, 7, plane, 0)
    lax.fori_loop(2, 6, along_x, 0)
    for copy in halos + more:
        copy.wait()

    def rest(e, _):
        at = 9 * e
        for row in range(0, 128, STRIP):
            flux_x[at, pl.ds(row, STRIP), :] = local_parts(dens, at + 1, row + 16, STRIP)[2]
        plane(7 * e, 0)
        along_x(6 * e, 0)
        along_x(6 * e + 1, 0)
        return 0

    lax.fori_loop(0, 2, rest, 0)


def potential(occupation, live, index, proj, core, orbitals):
    tiles = orbitals.reshape(2, 8, 64, 8, 4, 128).transpose(0, 1, 2, 4, 3, 5).reshape(2, 8, 256, 8, 128)
    core = core.reshape(8, 16, 8, 4, 128).transpose(0, 1, 3, 2, 4).reshape(8, 64, 8, 128)
    both = pltpu.VMEM((2, 4, 33, 4, 8, 128), f32)
    strengths = pltpu.VMEM((8, 128), f32)
    points = pltpu.VMEM((64, 128), i32)
    dma = pltpu.SemaphoreType.DMA
    return pl.pallas_call(
        potential_kernel,
        in_specs=[SM, SM, VM, VM, VM, HBM],
        out_specs=VM,
        out_shape=jax.ShapeDtypeStruct((8, 128, 512), f32),
        scratch_shapes=[
            pltpu.VMEM((2048, 2, 8, 128), f32),
            pltpu.VMEM((256 * STEP, 128), f32),
            pltpu.VMEM((256 * STEP, 128), f32),
            pltpu.VMEM((128, 128), f32),
            pltpu.VMEM((12, 160, 512), f32),
            pltpu.VMEM((10, 128, 512), f32),
            pltpu.VMEM((160, 512), f32),
            both,
            both,
            both,
            pltpu.VMEM((4, 33, 4, 8, 128), f32),
            strengths,
            strengths,
            pltpu.VMEM((2, 8, 128), f32),
            points,
            pltpu.SMEM((64, 128), i32),
            pltpu.VMEM((64, 8, 128), f32),
            points,
            pltpu.VMEM((64, 128), f32),
            pltpu.VMEM((256, 8192), bf16),
            dma((1,)),
            dma((16,)),
            dma((8,)),
            dma((8,)),
            dma((8,)),
            dma((8,)),
            dma((2,)),
            dma((2,)),
            dma((4,)),
            dma((4,)),
        ],
        compiler_params=pltpu.CompilerParams(
            vmem_limit_bytes=60 * MIB, collective_id=0, has_side_effects=True
        ),
        cost_estimate=pl.CostEstimate(flops=100 * MIB, bytes_accessed=40 * MIB, transcendentals=0),
        name="potential",
    )(occupation, live, index, proj, core, tiles)


def shards(orbitals, occupation, core_density, proj_values, block_index, live_points):
    return potential(
        occupation, live_points, block_index, proj_values, core_density, orbitals
    )


def solution(mesh):
    placed = (
        P("band", "dom", None, None),
        P("band"),
        P("dom", "band", None),
        P("dom", None, None),
        P("dom", None),
        P("dom"),
    )
    return jax.shard_map(
        shards, mesh=mesh, in_specs=placed, out_specs=P("dom", "band", None), check_vma=False
    )
```

time: 92.9 us -> 87.6 us (0.943)
  starting transfers between devices: 6.31 us -> 0 us
  waiting for transfers between devices: 2.97 us -> 0 us
  local copies, waits for them, and re-layouts: 0.97 us -> 3.08 us
  Pallas kernels: 82.2 us -> 83.8 us
    ppermute x2 -> x0, starting transfers between devices: 6.31 us -> none  [the longest x1 4.75 us: shards(): above = lax.ppermute(d0, 'dom', [((i + 1) % 32, i) for i in range(32)])]
    ppermute x2 -> x0, waiting for transfers between devices: 2.97 us -> none  [the longest x1 2.97 us: shards(): below = lax.ppermute(d3, 'dom', [(i, (i + 1) % 32) for i in range(32)])]
    unnamed x4 -> x1, local copies, waits for them, and re-layouts: 0.97 us -> 3.08 us
    pallas_call x3 -> x1, Pallas kernels: 82.2 us -> 83.8 us  [potential(): pl.pallas_call(potential_kernel, in_specs=[SM, SM, VM, VM, VM, HBM], out_...]
  transfers between devices with their start and end apart: 2 -> 0, of which waited for: 1 -> 0; matrix products, arithmetic and copies ran while one was open for 0% -> 0% of each run, Pallas kernels for 10% -> 0%
where the time goes in v4:
time: 87.6 us; the launch traced here: 86.9 us
  Pallas kernels  83.8 us (96%)
  local copies, waits for them, and re-layouts  3.08 us (4%)
    pallas_call x1, Pallas kernels, potential(): pl.pallas_call(potential_kernel, in_specs=[SM, SM, VM, VM, VM, HBM], out_...  83.8 us
    unnamed x1, local copies, waits for them, and re-layouts  3.08 us

profile of v4, /device:TPU:0, one launch (start us, length us, event | category | flops | bytes accessed | tf_op | source)
XLA Modules:
  0.0 86.9 jit_solution(15949667454027518788)
XLA Ops:
  0.0 83.8 %potential.1 = f32[8,128,512]{2,1,0:T(8,128)} custom-call(s32[2]{0:T(128)} %occupation.1, s32[64]{0:T(128)} %live.1, s32[64,128]{1,0:T(8,128)} %index.1, f32[64,8,128]{2,1,0:T(8,128)} %proj.1, f32[8,64,8,128]{3,2,1,0:T(8,128)} %bitcast.11, f32[2,8,256,8,128]{4,3,2,1,0:T(8,128)} %bitcast.10), custom_call_target="tpu_custom_call" | custom-call | flops 104857600 | bytes 41943040 | tf_op jit(solution)/shard_map/potential/pallas_call | solution.py:420
  83.8 3.1 %copy.8 = f32[8,128,512]{2,1,0:T(8,128)} copy(f32[8,128,512]{2,1,0:T(8,128)} %potential.1) | data formatting | bytes 4194304

commit v5 on v4

--- a/solution.py
+++ b/solution.py
@@ -83,6 +83,7 @@
     pot_ref,
     buf, picked_a, picked_b, rims, dens, flux_x, flux_y, keep, send, recv, come, w_mine, w_core, w_come, rows_v, rows, beta, tile_of, row_of, vt,
     rows_sem, load_sem, swap_out, swap_in, far_out, far_in, w_out, w_in, halo_out, halo_in,
+    hop1, hop2, hop1_out, hop1_in, hop2_out, hop2_in, hop3_out, hop3_in, rim_out, rim_in,
 ):
     band = lax.axis_index("band")
     dom = lax.axis_index("dom")
@@ -109,8 +110,44 @@
         for copy in loads(gi):
             copy.start()
     barrier = pltpu.get_barrier_semaphore()
+    spot = lax.rem(dom, 16)
+    layer = dom - spot
+    in_last = spot >= 12
+    in_row = in_last | (spot < 4)
+    lane = jnp.where(in_last, spot - 12, spot)
+    row_first = jnp.where(in_last, layer + 12, layer)
+    sender = jnp.where(in_last, layer, layer + 15)
+    taker = jnp.where(in_last, layer + 15, layer)
+    far_first = jnp.where(in_last, layer, layer + 12)
+    is_last = spot == 15
+    is_first = spot == 0
+    is_end = is_last | is_first
+    other_layer = (band, lax.rem(dom + 16, 32))
+
+    def greet(partner):
+        pl.semaphore_signal(barrier, inc=1, device_id=partner, device_id_type=MESH)
+
     for partner in (mate, opposite, after, before):
-        pl.semaphore_signal(barrier, inc=1, device_id=partner, device_id_type=MESH)
+        greet(partner)
+
+    @pl.when(in_row)
+    def _():
+        greet(other_layer)
+        greet((band, sender))
+
+    @pl.when(in_row & jnp.logical_not(is_end))
+    def _():
+        greet((band, taker))
+
+    @pl.when(is_end)
+    def _():
+        for k in range(4):
+            greet((band, far_first + k))
+
+            @pl.when(lane != k)
+            def _():
+                greet((band, row_first + k))
+
     w0 = occupation[0].astype(f32) * 0.001
     w1 = occupation[1].astype(f32) * 0.001
 
@@ -194,7 +231,7 @@
                 copy.start()
         fill(send, gi, 0, False)
         if gi == 0:
-            pl.semaphore_wait(barrier, 4)
+            pl.semaphore_wait(barrier, jnp.where(is_end, 13, jnp.where(in_row, 7, 4)))
         swap(0, gi).start()
         fill(keep, gi, 0, True)
         fill(send, gi, 1, False)
@@ -268,9 +305,7 @@
     second = send_w(w_core, 1, opposite)
     second.start()
     across(1, 1).start()
-    for gi in range(2, 4):
-        for half in range(2):
-            across(gi, half).start()
+    across(2, 0).start()
     for gi in range(2, 4):
         swap(1, gi).wait()
         add_received(1, gi)
@@ -377,37 +412,149 @@
             )
         return 0
 
+    def remote(src, dst, out, came, partner):
+        return pltpu.make_async_remote_copy(
+            src_ref=src,
+            dst_ref=dst,
+            send_sem=out,
+            recv_sem=came,
+            device_id=partner,
+            device_id_type=MESH,
+        )
+
+    def part(plane, k):
+        return dens.at[pl.ds(plane, 2), pl.ds(pl.multiple_of(16 + 32 * k, 8), 32)]
+
+    gives = jnp.where(in_last, 8, 2)
+    lands = jnp.where(in_last, 10, 0)
+
+    def to_row(k):
+        return remote(part(gives, k), hop1, hop1_out.at[k], hop1_in.at[0], (band, far_first + k))
+
+    def across_to_row():
+        return remote(hop1, hop2, hop2_out.at[0], hop2_in.at[0], other_layer)
+
+    def across_to_taker():
+        return remote(hop1, part(lands, lane), hop2_out.at[0], hop3_in.at[lane], other_layer)
+
+    def to_taker():
+        return remote(hop2, part(lands, lane), hop3_out.at[0], hop3_in.at[lane], (band, taker))
+
+    def from_row(k):
+        return remote(hop2, part(lands, k), hop3_out.at[0], hop3_in.at[k], (band, taker))
+
+    def rim_copy(j):
+        here = pl.ds(8 + 136 * j, 8)
+        return remote(
+            dens.at[jnp.where(in_last, 9, 2), here],
+            dens.at[jnp.where(in_last, 1, 10), here],
+            rim_out.at[j],
+            rim_in.at[j],
+            (band, lax.rem(dom + jnp.where(in_last, 1, 31), 32)),
+        )
+
+    def send_by_parts():
+        for k in range(4):
+            to_row(k).start()
+        for j in range(2):
+            rim_copy(j).start()
+
+    def start(copies):
+        for copy in copies:
+            copy.start()
+
+    def arrived(copies):
+        for copy in copies:
+            copy.wait_recv()
+
+    to_before = [halo(0, 2, 10, 8, 144, before), halo(1, 3, 11, 16, 128, before)]
+    to_after = [halo(2, 9, 1, 8, 144, after), halo(3, 8, 0, 16, 128, after)]
     wait_far(0)
     density(0, True)
-    halos = [halo(0, 2, 10, 8, 144, before), halo(1, 3, 11, 16, 128, before)]
-    for copy in halos:
-        copy.start()
+    across(2, 1).start()
+    pl.when(is_first)(send_by_parts)
+    pl.when(jnp.logical_not(is_first))(lambda: start(to_before))
     wait_far(1)
     density(1, True)
-    more = [halo(2, 9, 1, 8, 144, after), halo(3, 8, 0, 16, 128, after)]
-    for copy in more:
-        copy.start()
+    across(3, 0).start()
+    pl.when(is_last)(send_by_parts)
+    pl.when(jnp.logical_not(is_last))(lambda: start(to_after))
     wait_far(2)
     density(2, True)
+
+    across(3, 1).start()
     lax.fori_loop(1, 3, plane, 0)
     density(3, False)
+
+    @pl.when(in_row)
+    def _():
+        to_row(0).wait_recv()
+
+        @pl.when(is_end)
+        def _():
+            across_to_taker().start()
+
+        @pl.when(jnp.logical_not(is_end))
+        def _():
+            across_to_row().start()
+
     wait_far(3)
     add_arrived(3)
-    lax.fori_loop(3, 7, plane, 0)
+    lax.fori_loop(3, 5, plane, 0)
+
+    @pl.when(in_row & jnp.logical_not(is_end))
+    def _():
+        across_to_row().wait_recv()
+        to_taker().start()
+
+    lax.fori_loop(5, 7, plane, 0)
     lax.fori_loop(2, 6, along_x, 0)
-    for copy in halos + more:
-        copy.wait()
-
-    def rest(e, _):
+
+    def rest(e):
         at = 9 * e
         for row in range(0, 128, STRIP):
             flux_x[at, pl.ds(row, STRIP), :] = local_parts(dens, at + 1, row + 16, STRIP)[2]
         plane(7 * e, 0)
         along_x(6 * e, 0)
         along_x(6 * e + 1, 0)
-        return 0
-
-    lax.fori_loop(0, 2, rest, 0)
+
+    def by_parts():
+        for j in range(2):
+            rim_copy(j).wait_recv()
+        for k in range(4):
+            from_row(k).wait_recv()
+
+    pl.when(is_first)(lambda: arrived(to_before))
+    pl.when(jnp.logical_not(is_first))(lambda: arrived(to_after))
+    rest(jnp.where(is_first, 1, 0))
+    pl.when(is_end)(by_parts)
+    pl.when(jnp.logical_not(is_end))(lambda: arrived(to_before))
+    rest(jnp.where(is_first, 0, 1))
+
+    @pl.when(jnp.logical_not(is_first))
+    def _():
+        for copy in to_before:
+            copy.wait_send()
+
+    @pl.when(jnp.logical_not(is_last))
+    def _():
+        for copy in to_after:
+            copy.wait_send()
+
+    @pl.when(in_row)
+    def _():
+        across_to_row().wait_send()
+
+    @pl.when(in_row & jnp.logical_not(is_end))
+    def _():
+        to_taker().wait_send()
+
+    @pl.when(is_end)
+    def _():
+        for j in range(2):
+            rim_copy(j).wait_send()
+        for k in range(4):
+            to_row(k).wait_send()
 
 
 def potential(occupation, live, index, proj, core, orbitals):
@@ -453,6 +600,16 @@
             dma((2,)),
             dma((4,)),
             dma((4,)),
+            pltpu.VMEM((2, 32, 512), f32),
+            pltpu.VMEM((2, 32, 512), f32),
+            dma((4,)),
+            dma((1,)),
+            dma((1,)),
+            dma((1,)),
+            dma((1,)),
+            dma((4,)),
+            dma((2,)),
+            dma((2,)),
         ],
         compiler_params=pltpu.CompilerParams(
             vmem_limit_bytes=60 * MIB, collective_id=0, has_side_effects=True

time: 87.6 us -> 79 us (0.902)
  Pallas kernels: 83.8 us -> 75.8 us
    pallas_call x1, Pallas kernels: 83.8 us -> 75.8 us  [potential(): pl.pallas_call(potential_kernel, in_specs=[SM, SM, VM, VM, VM, HBM], out_...]
where the time goes in v5:
time: 79 us; the launch traced here: 78.9 us
  Pallas kernels  75.8 us (96%)
  local copies, waits for them, and re-layouts  3.08 us (4%)
    pallas_call x1, Pallas kernels, potential(): pl.pallas_call(potential_kernel, in_specs=[SM, SM, VM, VM, VM, HBM], out_...  75.8 us
    unnamed x1, local copies, waits for them, and re-layouts  3.08 us

profile of v5, /device:TPU:0, one launch (start us, length us, event | category | flops | bytes accessed | tf_op | source)
XLA Modules:
  0.0 78.9 jit_solution(9076419221229666955)
XLA Ops:
  0.0 75.8 %potential.1 = f32[8,128,512]{2,1,0:T(8,128)} custom-call(s32[2]{0:T(128)} %occupation.1, s32[64]{0:T(128)} %live.1, s32[64,128]{1,0:T(8,128)} %index.1, f32[64,8,128]{2,1,0:T(8,128)} %proj.1, f32[8,64,8,128]{3,2,1,0:T(8,128)} %bitcast.11, f32[2,8,256,8,128]{4,3,2,1,0:T(8,128)} %bitcast.10), custom_call_target="tpu_custom_call" | custom-call | flops 104857600 | bytes 41943040 | tf_op jit(solution)/shard_map/potential/pallas_call | solution.py:567
  75.8 3.1 %copy.8 = f32[8,128,512]{2,1,0:T(8,128)} copy(f32[8,128,512]{2,1,0:T(8,128)} %potential.1) | data formatting | bytes 4194304

commit v6 on v5

--- a/solution.py
+++ b/solution.py
@@ -55,7 +55,7 @@
     return e_n, twice * gy, twice * gx, twice * gz
 
 
-STRIP = 16
+STRIP = 32
 
 
 def full_plane(dens, x, flux_y, put):
@@ -79,8 +79,9 @@
 
 
 def potential_kernel(
-    occupation, live, index, proj, core, orb,
+    occupation, live, index, proj_hbm, core_hbm, orb,
     pot_ref,
+    proj, core,
     buf, picked_a, picked_b, rims, dens, flux_x, flux_y, keep, send, recv, come, w_mine, w_core, w_come, rows_v, rows, beta, tile_of, row_of, vt,
     rows_sem, load_sem, swap_out, swap_in, far_out, far_in, w_out, w_in, halo_out, halo_in,
     hop1, hop2, hop1_out, hop1_in, hop2_out, hop2_in, hop3_out, hop3_in, rim_out, rim_in,
@@ -106,15 +107,18 @@
                 )
         return made
 
-    for gi in range(2):
-        for copy in loads(gi):
-            copy.start()
+    for copy in loads(0):
+        copy.start()
+    core_in = pltpu.make_async_copy(core_hbm, core, rows_sem.at[1])
+    proj_in = pltpu.make_async_copy(proj_hbm, proj, rows_sem.at[2])
+    core_in.start()
+    proj_in.start()
     barrier = pltpu.get_barrier_semaphore()
     spot = lax.rem(dom, 16)
     layer = dom - spot
     in_last = spot >= 12
-    in_row = in_last | (spot < 4)
     lane = jnp.where(in_last, spot - 12, spot)
+    in_row = (in_last & (lane != 1)) | ((spot < 4) & (lane != 2))
     row_first = jnp.where(in_last, layer + 12, layer)
     sender = jnp.where(in_last, layer, layer + 15)
     taker = jnp.where(in_last, layer + 15, layer)
@@ -139,14 +143,15 @@
     def _():
         greet((band, taker))
 
+    far_lanes = (jnp.where(in_last, 0, 3), jnp.where(in_last, 1, 2), jnp.where(in_last, 3, 0))
+    near_lanes = (jnp.where(in_last, 2, 1), jnp.where(in_last, 0, 3))
+
     @pl.when(is_end)
     def _():
-        for k in range(4):
+        for k in far_lanes:
             greet((band, far_first + k))
-
-            @pl.when(lane != k)
-            def _():
-                greet((band, row_first + k))
+        for k in near_lanes:
+            greet((band, row_first + k))
 
     w0 = occupation[0].astype(f32) * 0.001
     w1 = occupation[1].astype(f32) * 0.001
@@ -226,24 +231,29 @@
     for gi in range(4):
         for copy in loads(gi):
             copy.wait()
-        if gi < 2:
-            for copy in loads(gi + 2):
+        if gi < 3:
+            for copy in loads(gi + 1):
                 copy.start()
+        if gi == 0:
+            core_in.wait()
         fill(send, gi, 0, False)
         if gi == 0:
-            pl.semaphore_wait(barrier, jnp.where(is_end, 13, jnp.where(in_row, 7, 4)))
+            pl.semaphore_wait(barrier, jnp.where(is_end, 11, jnp.where(in_row, 7, 4)))
         swap(0, gi).start()
         fill(keep, gi, 0, True)
         fill(send, gi, 1, False)
         swap(1, gi).start()
-        fill(keep, gi, 1, True)
+        if gi > 0:
+            fill(keep, gi, 1, True)
         swap(0, gi).wait()
         add_received(0, gi)
         if gi < 2:
             across(gi, 0).start()
         if gi < 1:
             across(gi, 1).start()
-
+            fill(keep, gi, 1, True)
+
+    proj_in.wait()
     flat = buf.reshape(32768, 128)
     sub = lax.broadcasted_iota(i32, (128, 128), 0)
     two = lax.broadcasted_iota(i32, (256, 128), 0) - 2 * lax.broadcasted_iota(i32, (256, 128), 1)
@@ -327,41 +337,47 @@
 
     lax.fori_loop(0, 64 // STEP, spread_step, 0)
 
-    def spread_tile(t, count):
+    def spread_tiles(tiles, count):
         ids = lax.broadcasted_iota(i32, (count, 128), 0).astype(f32).astype(bf16)
-        acc = jnp.zeros((count, 256), f32)
+        acc = jnp.zeros((count * len(tiles), 256), f32)
         for q in range(8):
-            hots = []
-            for b in range(8 * q, 8 * q + 8):
-                at = jnp.where(tile_of[b : b + 1, :] == t, row_of[b : b + 1, :], -1.0).astype(bf16)
-                hots.append(jnp.where(at == ids, jnp.ones((), bf16), jnp.zeros((), bf16)))
+            strips = []
+            for t in tiles:
+                hots = []
+                for b in range(8 * q, 8 * q + 8):
+                    at = jnp.where(tile_of[b : b + 1, :] == t, row_of[b : b + 1, :], -1.0).astype(bf16)
+                    hots.append(jnp.where(at == ids, jnp.ones((), bf16), jnp.zeros((), bf16)))
+                strips.append(jnp.concatenate(hots, axis=1))
             acc = acc + lax.dot_general(
-                jnp.concatenate(hots, axis=1),
+                jnp.concatenate(strips, axis=0),
                 vt[:, 1024 * q : 1024 * q + 1024],
                 NT,
                 preferred_element_type=f32,
             )
         return acc[:, :128] + acc[:, 128:]
 
-    rims[...] = spread_tile(16, 128)
+    rims[...] = spread_tiles((16,), 128)
 
     def density(gi, arrived):
         at = 2 + 2 * ORDER[gi]
 
-        def columns(c, _):
-            cols = pl.ds(pl.multiple_of(128 * c, 128), 128)
-            sums = keep[1, gi, pl.ds(0, 33), c]
-            if arrived:
-                sums = sums + come[gi, pl.ds(0, 33), c]
-            body = spread_tile(4 * gi + c, 256) + sums[0:32].reshape(256, 128)
-            rim = rims[pl.ds(pl.multiple_of((4 * gi + c) * 8, 8), 8), :] + sums[32]
-            for i in range(2):
-                dens[at + i, 16:144, cols] = body[128 * i : 128 * i + 128]
-                dens[at + i, 14:16, cols] = rim[2 * i : 2 * i + 2]
-                dens[at + i, 144:146, cols] = rim[4 + 2 * i : 6 + 2 * i]
+        def columns(half, _):
+            both = spread_tiles((4 * gi + 2 * half, 4 * gi + 2 * half + 1), 256)
+            for j in range(2):
+                c = 2 * half + j
+                cols = pl.ds(pl.multiple_of(128 * c, 128), 128)
+                sums = keep[1, gi, pl.ds(0, 33), c]
+                if arrived:
+                    sums = sums + come[gi, pl.ds(0, 33), c]
+                body = both[256 * j : 256 * j + 256] + sums[0:32].reshape(256, 128)
+                rim = rims[pl.ds(pl.multiple_of((4 * gi + c) * 8, 8), 8), :] + sums[32]
+                for i in range(2):
+                    dens[at + i, 16:144, cols] = body[128 * i : 128 * i + 128]
+                    dens[at + i, 14:16, cols] = rim[2 * i : 2 * i + 2]
+                    dens[at + i, 144:146, cols] = rim[4 + 2 * i : 6 + 2 * i]
             return 0
 
-        lax.fori_loop(0, 4, columns, 0)
+        lax.fori_loop(0, 2, columns, 0)
 
     def add_arrived(gi):
         at = 2 + 2 * ORDER[gi]
@@ -428,17 +444,21 @@
     gives = jnp.where(in_last, 8, 2)
     lands = jnp.where(in_last, 10, 0)
 
+    piece = jnp.where(in_last, jnp.where(lane == 2, 2, 3), jnp.where(lane == 1, 2, 3))
+
     def to_row(k):
-        return remote(part(gives, k), hop1, hop1_out.at[k], hop1_in.at[0], (band, far_first + k))
+        slot = k % 2 if k < 2 else 0
+        target = (band, far_first + far_lanes[max(k - 1, 0)])
+        return remote(part(gives, k), hop1.at[slot], hop1_out.at[k], hop1_in.at[slot], target)
 
     def across_to_row():
-        return remote(hop1, hop2, hop2_out.at[0], hop2_in.at[0], other_layer)
-
-    def across_to_taker():
-        return remote(hop1, part(lands, lane), hop2_out.at[0], hop3_in.at[lane], other_layer)
+        return remote(hop1.at[0], hop2, hop2_out.at[0], hop2_in.at[0], other_layer)
+
+    def across_to_taker(k):
+        return remote(hop1.at[k], part(lands, k), hop2_out.at[k], hop3_in.at[k], other_layer)
 
     def to_taker():
-        return remote(hop2, part(lands, lane), hop3_out.at[0], hop3_in.at[lane], (band, taker))
+        return remote(hop2, part(lands, piece), hop3_out.at[0], hop3_in.at[piece], (band, taker))
 
     def from_row(k):
         return remote(hop2, part(lands, k), hop3_out.at[0], hop3_in.at[k], (band, taker))
@@ -486,17 +506,16 @@
     lax.fori_loop(1, 3, plane, 0)
     density(3, False)
 
-    @pl.when(in_row)
+    @pl.when(is_end)
+    def _():
+        for k in range(2):
+            to_row(k).wait_recv()
+            across_to_taker(k).start()
+
+    @pl.when(in_row & jnp.logical_not(is_end))
     def _():
         to_row(0).wait_recv()
-
-        @pl.when(is_end)
-        def _():
-            across_to_taker().start()
-
-        @pl.when(jnp.logical_not(is_end))
-        def _():
-            across_to_row().start()
+        across_to_row().start()
 
     wait_far(3)
     add_arrived(3)
@@ -541,18 +560,17 @@
         for copy in to_after:
             copy.wait_send()
 
-    @pl.when(in_row)
+    @pl.when(in_row & jnp.logical_not(is_end))
     def _():
         across_to_row().wait_send()
-
-    @pl.when(in_row & jnp.logical_not(is_end))
-    def _():
         to_taker().wait_send()
 
     @pl.when(is_end)
     def _():
         for j in range(2):
             rim_copy(j).wait_send()
+        for k in range(2):
+            across_to_taker(k).wait_send()
         for k in range(4):
             to_row(k).wait_send()
 
@@ -566,10 +584,12 @@
     dma = pltpu.SemaphoreType.DMA
     return pl.pallas_call(
         potential_kernel,
-        in_specs=[SM, SM, VM, VM, VM, HBM],
+        in_specs=[SM, SM, VM, HBM, HBM, HBM],
         out_specs=VM,
         out_shape=jax.ShapeDtypeStruct((8, 128, 512), f32),
         scratch_shapes=[
+            pltpu.VMEM((64, 8, 128), f32),
+            pltpu.VMEM((8, 64, 8, 128), f32),
             pltpu.VMEM((2048, 2, 8, 128), f32),
             pltpu.VMEM((256 * STEP, 128), f32),
             pltpu.VMEM((256 * STEP, 128), f32),
@@ -590,7 +610,7 @@
             points,
             pltpu.VMEM((64, 128), f32),
             pltpu.VMEM((256, 8192), bf16),
-            dma((1,)),
+            dma((3,)),
             dma((16,)),
             dma((8,)),
             dma((8,)),
@@ -600,11 +620,11 @@
             dma((2,)),
             dma((4,)),
             dma((4,)),
-            pltpu.VMEM((2, 32, 512), f32),
+            pltpu.VMEM((2, 2, 32, 512), f32),
             pltpu.VMEM((2, 32, 512), f32),
             dma((4,)),
-            dma((1,)),
-            dma((1,)),
+            dma((2,)),
+            dma((2,)),
             dma((1,)),
             dma((1,)),
             dma((4,)),

time: 79 us -> 75.3 us (0.953)
  Pallas kernels: 75.8 us -> 72 us
    pallas_call x1, Pallas kernels: 75.8 us -> 72 us  [potential(): pl.pallas_call(potential_kernel, in_specs=[SM, SM, VM, HBM, HBM, HBM], ou...]
where the time goes in v6:
time: 75.3 us; the launch traced here: 75.1 us
  Pallas kernels  72 us (96%)
  local copies, waits for them, and re-layouts  3.08 us (4%)
    pallas_call x1, Pallas kernels, potential(): pl.pallas_call(potential_kernel, in_specs=[SM, SM, VM, HBM, HBM, HBM], ou...  72 us
    unnamed x1, local copies, waits for them, and re-layouts  3.08 us

profile of v6, /device:TPU:0, one launch (start us, length us, event | category | flops | bytes accessed | tf_op | source)
XLA Modules:
  0.0 75.1 jit_solution(602738276146372397)
XLA Ops:
  0.0 72.0 %potential.1 = f32[8,128,512]{2,1,0:T(8,128)} custom-call(s32[2]{0:T(128)} %occupation.1, s32[64]{0:T(128)} %live.1, s32[64,128]{1,0:T(8,128)} %index.1, f32[64,8,128]{2,1,0:T(8,128)} %proj_hbm.1, f32[8,64,8,128]{3,2,1,0:T(8,128)} %bitcast.11, f32[2,8,256,8,128]{4,3,2,1,0:T(8,128)} %bitcast.10), custom_call_target="tpu_custom_call" | custom-call | flops 104857600 | bytes 41943040 | tf_op jit(solution)/shard_map/potential/pallas_call | solution.py:585
  72.0 3.1 %copy.8 = f32[8,128,512]{2,1,0:T(8,128)} copy(f32[8,128,512]{2,1,0:T(8,128)} %potential.1) | data formatting | bytes 4194304

commit v7 on v6

--- a/solution.py
+++ b/solution.py
@@ -519,14 +519,14 @@
 
     wait_far(3)
     add_arrived(3)
-    lax.fori_loop(3, 5, plane, 0)
+    plane(3, 0)
 
     @pl.when(in_row & jnp.logical_not(is_end))
     def _():
         across_to_row().wait_recv()
         to_taker().start()
 
-    lax.fori_loop(5, 7, plane, 0)
+    lax.fori_loop(4, 7, plane, 0)
     lax.fori_loop(2, 6, along_x, 0)
 
     def rest(e):

time: 75.3 us -> 75.3 us (level)
  no operation moved by 1% of the time
where the time goes in v7:
time: 75.3 us; the launch traced here: 75.1 us
  Pallas kernels  72 us (96%)
  local copies, waits for them, and re-layouts  3.08 us (4%)
    pallas_call x1, Pallas kernels, potential(): pl.pallas_call(potential_kernel, in_specs=[SM, SM, VM, HBM, HBM, HBM], ou...  72 us
    unnamed x1, local copies, waits for them, and re-layouts  3.08 us

profile of v7, /device:TPU:0, one launch (start us, length us, event | category | flops | bytes accessed | tf_op | source)
XLA Modules:
  0.0 75.1 jit_solution(7752948065162873697)
XLA Ops:
  0.0 72.0 %potential.1 = f32[8,128,512]{2,1,0:T(8,128)} custom-call(s32[2]{0:T(128)} %occupation.1, s32[64]{0:T(128)} %live.1, s32[64,128]{1,0:T(8,128)} %index.1, f32[64,8,128]{2,1,0:T(8,128)} %proj_hbm.1, f32[8,64,8,128]{3,2,1,0:T(8,128)} %bitcast.11, f32[2,8,256,8,128]{4,3,2,1,0:T(8,128)} %bitcast.10), custom_call_target="tpu_custom_call" | custom-call | flops 104857600 | bytes 41943040 | tf_op jit(solution)/shard_map/potential/pallas_call | solution.py:585
  72.0 3.1 %copy.8 = f32[8,128,512]{2,1,0:T(8,128)} copy(f32[8,128,512]{2,1,0:T(8,128)} %potential.1) | data formatting | bytes 4194304
